TPU v7x, 32 devices: a whole 2x2x4 slice. The times are simulated.
32 devices in a mesh: sec: 4 (over y, x), row: 2 (over core), col: 4 (over z).
Axes of the slice: x: 2, y: 2, z: 4, core: 2. Of those that a mesh axis runs over, the one named last changes fastest.
Arguments:
- rhs: float32 [4, 8192, 256], P('sec', ('row', 'col')), may hold values from -6 to 6
- inv_factor: float32 [4, 8192, 8192], P('sec', 'col', 'row')
- coupling: float32 [4, 8192, 8192], P('sec', 'row', 'col'), may hold values from -0.0625 to 0.0625
- pattern: int32 [4, 64, 64], P('sec', 'row', 'col'), may hold values 0 or 1
Outputs:
- solution: float32 [4, 8192, 256], P('sec', 'col')
- outgoing: float32 [4, 8192, 256], P('sec', ('row', 'col'))
All inputs are finite; a program needn't handle non-finite values. No bound on the sum of `pattern` on one device may be relied on, other than what follows from the above.
Results may differ from a plain program's by a relative error of at most 0.0001.
Values sent between devices are 32-bit elements; how exact they have to be, the bound alone decides.
No kernel may reach another device: no remote copies, remote signals or barrier semaphores. Data moves between devices by JAX's collectives and lax.ppermute only.
A program may use at most 192 MiB of HBM per device.

v0:
```python
import jax
import jax.numpy as jnp
from jax import lax
from jax.sharding import PartitionSpec as P


def shards(rhs, inv_factor, coupling, pattern):
    highest = lax.Precision.HIGHEST
    factor = inv_factor[0]
    coupling_local = coupling[0]
    occupancy = pattern[0].astype(jnp.float32)
    block_rows = coupling_local.shape[0] // occupancy.shape[0]
    block_cols = coupling_local.shape[1] // occupancy.shape[1]
    masked = (
        coupling_local.reshape(occupancy.shape[0], block_rows, occupancy.shape[1], block_cols)
        * occupancy[:, None, :, None]
    ).reshape(coupling_local.shape)
    parent_flag = lax.axis_index("sec") == lax.axis_size("sec") - 1
    rows_full = lax.all_gather(rhs[0], "col", axis=0, tiled=True)

    def solve_section(operand):
        shares = lax.psum_scatter(
            jnp.dot(factor, operand, precision=highest, preferred_element_type=jnp.float32),
            "row",
            scatter_dimension=0,
            tiled=True,
        )
        return lax.all_gather(shares, "row", axis=0, tiled=True)

    def run_segment(operand, with_total):
        solved = solve_section(operand)
        update = jnp.dot(masked, solved, precision=highest, preferred_element_type=jnp.float32)
        shares = lax.psum_scatter(update, "col", scatter_dimension=0, tiled=True)
        child_sum = None
        if with_total:
            child_sum = lax.psum(jnp.where(parent_flag, 0.0, update), ("sec", "col"))
        return (solved, shares, child_sum)

    solved_a, shares_a, total_a = run_segment(rows_full, True)
    solved_b, shares_b, unused = run_segment(rows_full - total_a, False)
    solution = jnp.where(parent_flag, solved_b, solved_a)
    outgoing = jnp.where(parent_flag, shares_b, shares_a)
    return (solution[None], outgoing[None])


def solution(mesh):
    placed = (
        P("sec", ("row", "col"), None),
        P("sec", "col", "row"),
        P("sec", "row", "col"),
        P("sec", "row", "col"),
    )
    return jax.shard_map(
        shards,
        mesh=mesh,
        in_specs=placed,
        out_specs=(P("sec", "col", None), P("sec", ("row", "col"), None)),
        check_vma=False,
    )
```

profile of v0, /device:TPU:14, one launch (start us, length us, event | category | flops | bytes accessed | tf_op | source)
XLA Modules:
  0.0 602.8 jit_solution(7347920608005669970)
XLA Ops:
  7.2 0.7 all-gather.9.cloned.1.call-update
  7.9 0.0 reduce-scatter.5.cloned.1.call-start
  8.0 81.1 %all-gather.9.cloned.1.call-done = f32[1,4096,256]{2,1,0:T(8,128)} async-done(((f32[1,1024,256]{2,1,0:T(8,128)}), f32[1,4096,256]{2,1,0:T(8,128)}) %all-gather.9.cloned.1.call-update) | async-done | bytes 4194320 | tf_op jit(solution)/shard_map/all_gather | solution.py:19
  89.0 31.4 %fusion.2 = f32[2048,256]{1,0:T(8,128)} fusion(f32[1,2048,4096]{2,1,0:T(8,128)} %param.5, f32[1,4096,256]{2,1,0:T(8,128)} %all-gather.9.cloned.1.call-done), kind=kOutput, calls=%fused_computation.3 | convolution fusion | flops 25769803776 | bytes 39845888 | tf_op jit(solution)/shard_map/dot_general | solution.py:23
  120.5 0.0 all-gather.5.cloned.1.call-start
  120.5 11.0 %reduce-scatter.5.cloned.1.call-done = f32[1024,256]{1,0:T(8,128)} async-done(((f32[2048,256]{1,0:T(8,128)}), f32[1024,256]{1,0:T(8,128)}) %reduce-scatter.5.cloned.1.call-update) | async-done | bytes 1048592 | tf_op jit(solution)/shard_map/reduce_scatter | solution.py:22
  131.5 0.2 all-reduce.2.cloned.1.call-start
  131.8 0.1 copy.6
  131.8 13.1 %all-gather.5.cloned.1.call-done = f32[2048,256]{1,0:T(8,128)} async-done(((f32[1024,256]{1,0:T(8,128)}), f32[2048,256]{1,0:T(8,128)}) %all-gather.5.cloned.1.call-update) | async-done | bytes 2097168 | tf_op jit(solution)/shard_map/all_gather | solution.py:28
  144.9 11.1 %mul.11 = f32[32,128,16,128]{3,2,1,0:T(8,128)} broadcast(f32[32,16]{1,0:T(8,128)S(1)} %copy.6), dimensions={0,2} | broadcast | bytes 33556480 | tf_op jit(solution)/shard_map/mul | solution.py:15
  156.0 44.2 %broadcast_select_fusion = (f32[4096,256]{1,0:T(8,128)}, f32[4096,256]{1,0:T(8,128)}) fusion(pred[]{:T(512)S(6)} %eq.3, f32[2048,256]{1,0:T(8,128)S(1)} %copy-done, f32[512,8,16,128]{3,2,1,0:T(8,128)} %bitcast.38, f32[1,4096,2048]{2,1,0:T(8,128)} %param.6), kind=kOutput, calls=%fused_computation.11 | convolution fusion | flops 25779240960 | bytes 77594624 | tf_op jit(solution)/shard_map/dot_general | solution.py:32
  200.3 0.3 reduce-scatter.7.cloned.1.call-start
  200.6 167.5 %all-reduce.2.cloned.1.call-done = f32[4096,256]{1,0:T(8,128)} async-done(((f32[4096,256]{1,0:T(8,128)}), f32[4096,256]{1,0:T(8,128)}) %all-reduce.2.cloned.1.call-update) | async-done | bytes 4194320 | tf_op jit(solution)/shard_map/psum | solution.py:36
  368.1 42.1 %fusion.7 = f32[2048,256]{1,0:T(8,128)} fusion(f32[1,2048,4096]{2,1,0:T(8,128)} %param.5, f32[4096,256]{1,0:T(8,128)} %all-reduce.2.cloned.1.call-done, f32[1,4096,256]{2,1,0:T(8,128)} %all-gather.9.cloned.1.call-done), kind=kOutput, calls=%fused_computation.9 | convolution fusion | flops 25770852352 | bytes 44040192 | tf_op jit(solution)/shard_map/dot_general | solution.py:23
  410.3 0.0 all-gather.7.cloned.1.call-start
  410.3 10.3 %reduce-scatter.7.cloned.1.call-done = f32[1024,256]{1,0:T(8,128)} async-done(((f32[2048,256]{1,0:T(8,128)}), f32[1024,256]{1,0:T(8,128)}) %reduce-scatter.7.cloned.1.call-update) | async-done | bytes 1048592 | tf_op jit(solution)/shard_map/reduce_scatter | solution.py:22
  420.7 0.7 reduce-scatter.11.cloned.1.call-update
  421.4 0.0 reduce-scatter.9.cloned.1.call-start
  421.5 12.5 %all-gather.7.cloned.1.call-done = f32[2048,256]{1,0:T(8,128)} async-done(((f32[1024,256]{1,0:T(8,128)}), f32[2048,256]{1,0:T(8,128)}) %all-gather.7.cloned.1.call-update) | async-done | bytes 2097168 | tf_op jit(solution)/shard_map/all_gather | solution.py:28
  433.9 44.3 %fusion.4 = f32[4096,256]{1,0:T(8,128)} fusion(f32[2048,256]{1,0:T(8,128)} %all-gather.7.cloned.1.call-done, f32[512,8,16,128]{3,2,1,0:T(8,128)} %bitcast.39, f32[1,4096,2048]{2,1,0:T(8,128)} %param.6), kind=kOutput, calls=%fused_computation.5 | convolution fusion | flops 25778192384 | bytes 73400320 | tf_op jit(solution)/shard_map/dot_general | solution.py:32
  478.3 3.2 select_bitcast_fusion
  481.5 32.5 %reduce-scatter.11.cloned.1.call-done = f32[1024,256]{1,0:T(8,128)} async-done(((f32[4096,256]{1,0:T(8,128)}), f32[1024,256]{1,0:T(8,128)}) %reduce-scatter.11.cloned.1.call-update) | async-done | bytes 1048592 | tf_op jit(solution)/shard_map/reduce_scatter | solution.py:33
  514.0 79.6 %reduce-scatter.9.cloned.1.call-done = f32[1024,256]{1,0:T(8,128)} async-done(((f32[4096,256]{1,0:T(8,128)}), f32[1024,256]{1,0:T(8,128)}) %reduce-scatter.9.cloned.1.call-update) | async-done | bytes 1048592 | tf_op jit(solution)/shard_map/reduce_scatter | solution.py:33
  593.6 2.3 select_bitcast_fusion.1
  (13 shorter events, 0.2 us)
Async XLA Ops:
  7.2 81.8 %all-gather.9.cloned.1.call-start = ((), (), s32[]{:S(2)}) async-start(), calls=%async_computation.11 | async-start | bytes 5242880 | tf_op jit(solution)/shard_map/all_gather | solution.py:19
  7.9 123.8 %copy-start.1 = (s32[1,32,16]{1,2,0:T(8,128)S(1)}, s32[1,32,16]{1,2,0:T(8,128)}, u32[]{:S(2)}) copy-start(s32[1,32,16]{1,2,0:T(8,128)} %param.7) | copy-start | bytes 6148
  7.9 123.6 %reduce-scatter.5.cloned.1.call-start = ((), (), s32[]{:S(2)}) async-start(), calls=%async_computation.4 | async-start | bytes 3145728 | tf_op jit(solution)/shard_map/reduce_scatter | solution.py:22
  120.5 24.4 %all-gather.5.cloned.1.call-start = ((), (), s32[]{:S(2)}) async-start(), calls=%async_computation.5 | async-start | bytes 3145728 | tf_op jit(solution)/shard_map/all_gather | solution.py:28
  131.5 236.6 %all-reduce.2.cloned.1.call-start = ((), (), s32[]{:S(2)}) async-start(), calls=%async_computation.6 | async-start | bytes 8388608 | tf_op jit(solution)/shard_map/psum | solution.py:36
  144.9 11.1 %copy-start = (f32[2048,256]{1,0:T(8,128)S(1)}, f32[2048,256]{1,0:T(8,128)}, u32[]{:S(2)}) copy-start(f32[2048,256]{1,0:T(8,128)} %all-gather.5.cloned.1.call-done) | copy-start | bytes 6291460
  200.3 220.3 %reduce-scatter.7.cloned.1.call-start = ((), (), s32[]{:S(2)}) async-start(), calls=%async_computation.7 | async-start | bytes 3145728 | tf_op jit(solution)/shard_map/reduce_scatter | solution.py:22
  410.3 23.7 %all-gather.7.cloned.1.call-start = ((), (), s32[]{:S(2)}) async-start(), calls=%async_computation.8 | async-start | bytes 3145728 | tf_op jit(solution)/shard_map/all_gather | solution.py:28
  420.7 93.3 %reduce-scatter.11.cloned.1.call-start = ((), (), s32[]{:S(2)}) async-start(), calls=%async_computation.10 | async-start | bytes 5242880 | tf_op jit(solution)/shard_map/reduce_scatter | solution.py:33
  421.4 172.2 %reduce-scatter.9.cloned.1.call-start = ((), (), s32[]{:S(2)}) async-start(), calls=%async_computation.9 | async-start | bytes 5242880 | tf_op jit(solution)/shard_map/reduce_scatter | solution.py:33
Sparse Core Ops, SparseCore 0:
  9.6 79.3 all-gather.8
  120.6 10.8 reduce-scatter.4
  133.1 11.7 all-gather.4
  200.4 167.6 all-reduce.1
  410.4 10.2 reduce-scatter.6
  422.1 11.7 all-gather.6
  436.3 77.6 reduce-scatter.10
  516.3 77.2 reduce-scatter.8
where the time goes:
time: 605 us; the launch traced here: 603 us
  waiting for transfers between devices  409 us (68%)
  matrix products  162 us (27%)
  between operations  14.2 us (2%)
  local copies, waits for them, and re-layouts  11.2 us (2%)
    psum x1, waiting for transfers between devices, run_segment(): child_sum = lax.psum(jnp.where(parent_flag, 0.0, update), ('sec', 'col'))  168 us
    reduce_scatter x2, waiting for transfers between devices, run_segment(): shares = lax.psum_scatter(update, 'col', scatter_dimension=0, tiled=True)  112 us
    dot_general x2, matrix products, run_segment(): jnp.dot(masked, solved, precision=highest, preferred_element_type=jnp.flo...  88.6 us
    all_gather x1, waiting for transfers between devices, shards(): rows_full = lax.all_gather(rhs[0], 'col', axis=0, tiled=True)  81.1 us
    dot_general x2, matrix products, solve_section(): jnp.dot(factor, operand, precision=highest, preferred_element_type=jnp.fl...  73.6 us
    all_gather x2, waiting for transfers between devices, solve_section(): return lax.all_gather(shares, 'row', axis=0, tiled=True)  25.5 us
    reduce_scatter x2, waiting for transfers between devices, solve_section(): lax.psum_scatter(jnp.dot(factor, operand, precision=highest, preferred_el...  21.3 us
  transfers between devices with their start and end apart: 8, of which 8 were waited for; matrix products, arithmetic and copies ran while one was open for 8% of the time, Pallas kernels for 0%

commit v1 on v0

v1 whole, which is shorter than its diff:
```python
import functools

import jax
import jax.numpy as jnp
from jax import lax
from jax.experimental import pallas as pl
from jax.experimental.pallas import tpu as pltpu
from jax.sharding import PartitionSpec as P

F32 = jnp.float32
BF16 = jnp.bfloat16
AXES = ("sec", "col")
VMEM_LIMIT = 20 * 1024 * 1024
AT_END, ORDER, SHARD = 2, 3, 7
COST = pl.CostEstimate(flops=1, bytes_accessed=1, transcendentals=0)


def split_words(value):
    high = value.astype(BF16)
    low = (value - high.astype(F32)).astype(BF16)
    return high, low


def three_term(tile, words, width):
    high, low = split_words(tile)
    both = jnp.dot(high, words, preferred_element_type=F32) + jnp.dot(low, words, preferred_element_type=F32)
    return both[:, :width] + both[:, width:]


def pieces_body(role, pieces_at, counts, started, meta, factor_ref, *refs):
    n_ops = sum(counts)
    ops, refs = refs[:n_ops], refs[n_ops:]
    if started:
        total_ref, refs = refs[0], refs[1:]
    out_ref, panel, held, words, sums, panel_sem, op_sem, sum_sem, out_sem = refs
    pieces = len(counts)
    slots, tile, joined = panel.shape
    tiles = factor_ref.shape[0] // tile
    depth, width = joined // pieces, held.shape[2]

    @pl.when(meta[role] == 1)
    def _():
        def tile_copy(p, t):
            column = meta[ORDER + pieces_at[p]] * depth
            return pltpu.make_async_copy(
                factor_ref.at[
                    pl.ds(pl.multiple_of(t * tile, tile), tile),
                    pl.ds(pl.multiple_of(column, depth), depth),
                ],
                panel.at[t % slots, :, pl.ds(p * depth, depth)],
                panel_sem.at[p, t % slots],
            )

        at = 0
        for p, count in enumerate(counts):
            group = [pltpu.make_async_copy(ops[at + k], held.at[p], op_sem.at[p]) for k in range(count)]
            at += count
            if count == 1:
                group[0].start()
            else:

                @pl.when(meta[AT_END] == 0)
                def _():
                    group[0].start()

                @pl.when(meta[AT_END] == 1)
                def _():
                    group[1].start()

        if started:
            sum_copy = pltpu.make_async_copy(total_ref, sums, sum_sem)
            sum_copy.start()
        for t in range(slots):
            for p in range(pieces):
                tile_copy(p, t).start()
        for p in range(pieces):
            pltpu.make_async_copy(ops[0], held.at[p], op_sem.at[p]).wait()
            high, low = split_words(held[p])
            words[p * depth : (p + 1) * depth, :width] = high
            words[p * depth : (p + 1) * depth, width:] = low
        if started:
            sum_copy.wait()

        def out_copy(t):
            rows = pl.ds(pl.multiple_of(t * tile, tile), tile)
            return pltpu.make_async_copy(sums.at[rows], out_ref.at[rows], out_sem.at[t])

        @pl.loop(0, tiles)
        def _(t):
            rows = pl.ds(pl.multiple_of(t * tile, tile), tile)
            for p in range(pieces):
                tile_copy(p, t).wait()
            value = three_term(panel[t % slots], words[...], width)
            sums[rows, :] = value + sums[rows, :] if started else value
            out_copy(t).start()

            @pl.when(t + slots < tiles)
            def _():
                for p in range(pieces):
                    tile_copy(p, t + slots).start()

        for t in range(tiles):
            out_copy(t).wait()


def factor_pieces(role, meta, pieces_at, factor, operands, total):
    rows = factor.shape[0]
    depth, width = operands[0][0].shape
    counts = tuple(len(group) for group in operands)
    n_pieces = len(counts)
    tile = min(rows, 256)
    tiles = rows // tile
    started = total is not None
    slots = min(tiles, 4)
    flat = [ref for group in operands for ref in group] + ([total] if started else [])
    anywhere = pl.BlockSpec(memory_space=pl.ANY)
    return pl.pallas_call(
        functools.partial(pieces_body, role, pieces_at, counts, started),
        out_shape=jax.ShapeDtypeStruct((rows, width), F32),
        in_specs=[pl.BlockSpec(memory_space=pltpu.SMEM)] + [anywhere] * (1 + len(flat)),
        out_specs=anywhere,
        scratch_shapes=[
            pltpu.VMEM((slots, tile, n_pieces * depth), F32),
            pltpu.VMEM((n_pieces, depth, width), F32),
            pltpu.VMEM((n_pieces * depth, 2 * width), BF16),
            pltpu.VMEM((rows, width), F32),
            pltpu.SemaphoreType.DMA((n_pieces, slots)),
            pltpu.SemaphoreType.DMA((n_pieces,)),
            pltpu.SemaphoreType.DMA,
            pltpu.SemaphoreType.DMA((tiles,)),
        ],
        compiler_params=pltpu.CompilerParams(vmem_limit_bytes=VMEM_LIMIT),
        cost_estimate=COST,
    )(meta, factor, *flat)


def masked_terms(panel, mask_ref, words, base, block_rows, width):
    parts = []
    for j in range(panel.shape[0] // block_rows):
        block = panel[j * block_rows : (j + 1) * block_rows, :] * mask_ref[pl.ds(base + j, 1), :]
        parts.append(three_term(block, words, width))
    return parts


def first_body(
    role, meta, panel_ref, mask_ref, mine_ref, other_ref, solved_ref, words_ref, out_ref,
    panel, mask, held, words, sums, panel_sem, in_sem, solved_sem, words_sem, out_sem,
):
    tiles, tile, depth = panel.shape
    width = held.shape[2]
    block_rows = panel_ref.shape[0] // mask_ref.shape[0]
    per = tile // block_rows

    @pl.when(meta[role] == 1)
    def _():
        def tile_copy(t):
            rows = pl.ds(pl.multiple_of((meta[SHARD] * tiles + t) * tile, tile), tile)
            return pltpu.make_async_copy(panel_ref.at[rows], panel.at[t], panel_sem.at[t])

        def out_copy(t):
            rows = pl.ds(pl.multiple_of(t * tile, tile), tile)
            return pltpu.make_async_copy(sums.at[rows], out_ref.at[rows], out_sem.at[t])

        inputs = [
            pltpu.make_async_copy(mine_ref, held.at[0], in_sem.at[0]),
            pltpu.make_async_copy(other_ref, held.at[1], in_sem.at[1]),
            pltpu.make_async_copy(mask_ref, mask, in_sem.at[2]),
        ]
        for copy in inputs:
            copy.start()
        for t in range(tiles):
            tile_copy(t).start()
        for copy in inputs:
            copy.wait()
        solved = held[0] + held[1]
        held[0] = solved
        high, low = split_words(solved)
        words[:, :width] = high
        words[:, width:] = low
        solved_copy = pltpu.make_async_copy(held.at[0], solved_ref, solved_sem)
        words_copy = pltpu.make_async_copy(words, words_ref, words_sem)

        @pl.loop(0, tiles)
        def _(t):
            tile_copy(t).wait()
            parts = masked_terms(panel[t], mask, words[...], (meta[SHARD] * tiles + t) * per, block_rows, width)
            for j, part in enumerate(parts):
                sums[pl.ds(pl.multiple_of(t * tile + j * block_rows, block_rows), block_rows), :] = part
            out_copy(t).start()

        solved_copy.start()
        words_copy.start()
        for t in range(tiles):
            out_copy(t).wait()
        solved_copy.wait()
        words_copy.wait()


def panel_first(role, meta, n, panel, mask, mine, other):
    depth, width = mine.shape
    rows = panel.shape[0] // n
    tile = min(rows, 256)
    tiles = rows // tile
    anywhere = pl.BlockSpec(memory_space=pl.ANY)
    return pl.pallas_call(
        functools.partial(first_body, role),
        out_shape=(
            jax.ShapeDtypeStruct((depth, width), F32),
            jax.ShapeDtypeStruct((depth, 2 * width), BF16),
            jax.ShapeDtypeStruct((rows, width), F32),
        ),
        in_specs=[pl.BlockSpec(memory_space=pltpu.SMEM)] + [anywhere] * 4,
        out_specs=(anywhere,) * 3,
        scratch_shapes=[
            pltpu.VMEM((tiles, tile, depth), F32),
            pltpu.VMEM(mask.shape, F32),
            pltpu.VMEM((2, depth, width), F32),
            pltpu.VMEM((depth, 2 * width), BF16),
            pltpu.VMEM((rows, width), F32),
            pltpu.SemaphoreType.DMA((tiles,)),
            pltpu.SemaphoreType.DMA((3,)),
            pltpu.SemaphoreType.DMA,
            pltpu.SemaphoreType.DMA,
            pltpu.SemaphoreType.DMA((tiles,)),
        ],
        compiler_params=pltpu.CompilerParams(vmem_limit_bytes=VMEM_LIMIT),
        cost_estimate=COST,
    )(meta, panel, mask, mine, other)


def rest_body(role, meta, panel_ref, mask_ref, words_ref, *refs):
    n_out = len(refs) - 7
    outs = refs[:n_out]
    panel, mask, words, sums, panel_sem, in_sem, out_sem = refs[n_out:]
    slots, tile, depth = panel.shape
    width = words.shape[1] // 2
    rows = outs[0].shape[0]
    tiles = rows // tile
    block_rows = panel_ref.shape[0] // mask_ref.shape[0]
    per = tile // block_rows

    @pl.when(meta[role] == 1)
    def _():
        def tile_copy(k, t):
            at = pl.ds(pl.multiple_of((meta[SHARD + 1 + k] * tiles + t) * tile, tile), tile)
            slot = (k * tiles + t) % slots
            return pltpu.make_async_copy(panel_ref.at[at], panel.at[slot], panel_sem.at[slot])

        def out_copy(k, t):
            at = pl.ds(pl.multiple_of(t * tile, tile), tile)
            return pltpu.make_async_copy(sums.at[k, at], outs[k].at[at], out_sem.at[k, t])

        inputs = [
            pltpu.make_async_copy(words_ref, words, in_sem.at[0]),
            pltpu.make_async_copy(mask_ref, mask, in_sem.at[1]),
        ]
        for copy in inputs:
            copy.start()
        for n in range(slots):
            tile_copy(n // tiles, n % tiles).start()
        for copy in inputs:
            copy.wait()
        for k in range(n_out):

            @pl.loop(0, tiles)
            def _(t):
                tile_copy(k, t).wait()
                slot = (k * tiles + t) % slots
                parts = masked_terms(panel[slot], mask, words[...], (meta[SHARD + 1 + k] * tiles + t) * per, block_rows, width)
                for j, part in enumerate(parts):
                    sums[k, pl.ds(pl.multiple_of(t * tile + j * block_rows, block_rows), block_rows), :] = part
                out_copy(k, t).start()
                ahead = k + slots // tiles
                if ahead < n_out:
                    tile_copy(ahead, t).start()

        for k in range(n_out):
            for t in range(tiles):
                out_copy(k, t).wait()


def panel_rest(role, meta, n, panel, mask, words):
    depth, wide = words.shape
    width = wide // 2
    rows = panel.shape[0] // n
    tile = min(rows, 256)
    tiles = rows // tile
    anywhere = pl.BlockSpec(memory_space=pl.ANY)
    return pl.pallas_call(
        functools.partial(rest_body, role),
        out_shape=tuple(jax.ShapeDtypeStruct((rows, width), F32) for _ in range(n - 1)),
        in_specs=[pl.BlockSpec(memory_space=pltpu.SMEM)] + [anywhere] * 3,
        out_specs=(anywhere,) * (n - 1),
        scratch_shapes=[
            pltpu.VMEM((tiles, tile, depth), F32),
            pltpu.VMEM(mask.shape, F32),
            pltpu.VMEM((depth, wide), BF16),
            pltpu.VMEM((n - 1, rows, width), F32),
            pltpu.SemaphoreType.DMA((tiles,)),
            pltpu.SemaphoreType.DMA((2,)),
            pltpu.SemaphoreType.DMA((n - 1, tiles)),
        ],
        compiler_params=pltpu.CompilerParams(vmem_limit_bytes=VMEM_LIMIT),
        cost_estimate=COST,
    )(meta, panel, mask, words)


def send(value, secs, pairs):
    n = lax.axis_size("col")
    return lax.ppermute(value, AXES, [(s * n + a, s * n + b) for s in secs for a, b in pairs])


def hop(value, pairs):
    n = lax.axis_size("col")
    return lax.ppermute(value, AXES, [(a * n + c, b * n + c) for a, b in pairs for c in range(n)])


EDGES = ((0, 1), (1, 0), (2, 3), (3, 2))
MIDDLE = ((1, 2), (2, 1))
INWARD = ((1, 0), (2, 3))
OUTWARD = ((0, 1), (3, 2))
ARRIVE = ((0, 1, 2, 3), (1, 0, 2, 3), (2, 3, 1, 0), (3, 2, 1, 0))
LEAVE = ((3, 2, 1, 0), (3, 2, 0, 1), (0, 1, 3, 2), (0, 1, 2, 3))


class Order:
    def __init__(self):
        self.noted = ()

    def step(self, *operands):
        tied = lax.optimization_barrier((*operands, *self.noted))
        self.noted = ()
        return tied[: len(operands)]

    def note(self, *results):
        self.noted += results
        return results if len(results) > 1 else results[0]


class Line:
    def __init__(self, role, secs, meta, inner, factor, panel, mask):
        self.role, self.secs, self.meta, self.inner = role, secs, meta, inner
        self.factor, self.panel, self.mask = factor, panel, mask

    def send(self, value, pairs):
        return send(value, self.secs, pairs)

    def solve(self, pieces_at, operands, total):
        return factor_pieces(self.role, self.meta, pieces_at, self.factor, operands, total)

    def swap(self, value):
        return lax.ppermute(value, "row", [(0, 1), (1, 0)])

    def first(self, mine, other):
        return panel_first(self.role, self.meta, len(LEAVE), self.panel, self.mask, mine, other)

    def rest(self, words):
        return panel_rest(self.role, self.meta, len(LEAVE), self.panel, self.mask, words)

    def both(self, inner, end):
        return jnp.where(self.inner, inner, end)

    def pair(self, own_a, own_b, passed):
        order = Order()
        side_a, mid_a = order.note(self.send(own_a, EDGES), self.send(own_a, MIDDLE))
        order.note(self.meta, self.mask)
        mid_a, side_a, self.meta, self.mask = order.step(mid_a, side_a, self.meta, self.mask)
        near_a, across_a = order.note(self.send(mid_a, INWARD), self.send(side_a, MIDDLE))
        own_a, side_a, mid_a, near_a, across_a = order.step(own_a, side_a, mid_a, near_a, across_a)
        far_a = order.note(self.send(across_a, INWARD))
        tot_a = order.note(self.solve((0, 1, 2), [[own_a], [side_a], [mid_a, near_a]], None))
        own_b, tot_a, across_a, far_a = order.step(own_b(), tot_a, across_a, far_a)
        side_b, mid_b = order.note(self.send(own_b, EDGES), self.send(own_b, MIDDLE))
        tot_a = self.solve((3,), [[across_a, far_a]], tot_a)
        solved_a, words_a, r0_a = order.note(*self.first(tot_a, self.swap(tot_a)))
        mid_b, side_b, r0_a, words_a = order.step(mid_b, side_b, r0_a, words_a)
        near_b, across_b = order.note(self.send(self.both(mid_b, r0_a), EDGES), self.send(side_b, MIDDLE))
        r1_a, r2_a, rown_a = order.note(*self.rest(words_a))
        across_b, r0_a, r1_a, near_b, own_b, side_b, mid_b = order.step(
            across_b, r0_a, r1_a, near_b, own_b, side_b, mid_b
        )
        far_b = order.note(self.send(self.both(across_b, r1_a), EDGES))
        got_a = order.note(self.send(r0_a + near_b, MIDDLE))
        tot_b = order.note(self.solve((0, 1, 2), [[own_b], [side_b], [mid_b, near_b]], None))
        r2_a, got_a, r1_a, far_b, tot_b, across_b = order.step(r2_a, got_a, r1_a, far_b, tot_b, across_b)
        rs_a, rm_a = order.note(self.send(r2_a + got_a, EDGES), self.send(r1_a + far_b, MIDDLE))
        tot_b = self.solve((3,), [[across_b, far_b]], tot_b)
        solved_b, words_b, r0_b = order.note(*self.first(tot_b, self.swap(tot_b)))
        r0_b, words_b, rown_a, rs_a, rm_a = order.step(r0_b, words_b, rown_a, rs_a, rm_a)
        sent_a = rown_a + rs_a + rm_a
        near = order.note(self.send(r0_b, OUTWARD))
        passed_a = order.note(passed(sent_a))
        r1_b, r2_b, rown_b = order.note(*self.rest(words_b))
        r0_b, near, r1_b = order.step(r0_b, near, r1_b)
        far, got = order.note(self.send(r1_b, OUTWARD), self.send(r0_b + near, MIDDLE))
        r2_b, got, r1_b, far = order.step(r2_b, got, r1_b, far)
        rs_b, rm_b = self.send(r2_b + got, EDGES), self.send(r1_b + far, MIDDLE)
        sent_b = rown_b + rs_b + rm_b
        return solved_a, sent_a, solved_b, sent_b, passed_a


def to_last(sent):
    top = lax.axis_size("sec") - 1
    total = hop(sent, ((0, top),))
    for s in range(1, top):
        total = total + hop(sent, ((s, top),))
    return total


def shards_line(rhs, inv_factor, coupling, pattern):
    top = lax.axis_size("sec") - 1
    factor, panel = inv_factor[0], coupling[0]
    mask = jnp.repeat(pattern[0].astype(F32), panel.shape[1] // pattern.shape[2], axis=1)
    is_parent = lax.axis_index("sec") == top
    col = lax.axis_index("col")
    inner = (col != 0) & (col != lax.axis_size("col") - 1)
    flags = jnp.stack([~is_parent, is_parent, ~inner]).astype(jnp.int32)
    orders = jnp.asarray([a + b for a, b in zip(ARRIVE, LEAVE)], jnp.int32)
    meta = jnp.concatenate([flags, orders[col]])
    kids = Line(0, tuple(range(top)), meta, inner, factor, panel, mask)
    half = rhs.shape[2] // 2
    own = [rhs[0][:, :half], rhs[0][:, half:]]
    solved0, sent0, solved1, sent1, passed0 = kids.pair(own[0], lambda: own[1], to_last)
    head = Line(1, (top,), kids.meta, inner, factor, panel, kids.mask)
    psolved0, psent0, psolved1, psent1, _ = head.pair(
        own[0] - passed0, lambda: own[1] - to_last(sent1), lambda sent: sent
    )
    pick = lambda p, c: jnp.where(is_parent, p, c)
    solution = jnp.concatenate([pick(psolved0, solved0), pick(psolved1, solved1)], axis=1)
    outgoing = jnp.concatenate([pick(psent0, sent0), pick(psent1, sent1)], axis=1)
    return solution[None], outgoing[None]


def shards_any(rhs, inv_factor, coupling, pattern):
    highest = lax.Precision.HIGHEST
    factor = inv_factor[0]
    coupling_local = coupling[0]
    occupancy = pattern[0].astype(jnp.float32)
    block_rows = coupling_local.shape[0] // occupancy.shape[0]
    block_cols = coupling_local.shape[1] // occupancy.shape[1]
    masked = (
        coupling_local.reshape(occupancy.shape[0], block_rows, occupancy.shape[1], block_cols)
        * occupancy[:, None, :, None]
    ).reshape(coupling_local.shape)
    parent_flag = lax.axis_index("sec") == lax.axis_size("sec") - 1

    def segment(rows):
        operand = lax.all_gather(rows, "col", axis=0, tiled=True)
        solved = lax.psum(jnp.dot(factor, operand, precision=highest, preferred_element_type=F32), "row")
        update = jnp.dot(masked, solved, precision=highest, preferred_element_type=F32)
        return solved, lax.psum_scatter(update, "col", scatter_dimension=0, tiled=True)

    solved_a, shares_a = segment(rhs[0])
    total = lax.psum(jnp.where(parent_flag, 0.0, shares_a), "sec")
    solved_b, shares_b = segment(rhs[0] - total)
    solution = jnp.where(parent_flag, solved_b, solved_a)
    outgoing = jnp.where(parent_flag, shares_b, shares_a)
    return (solution[None], outgoing[None])


def solution(mesh):
    placed = (
        P("sec", ("row", "col"), None),
        P("sec", "col", "row"),
        P("sec", "row", "col"),
        P("sec", "row", "col"),
    )
    line = mesh.shape["col"] == 4 and mesh.shape["row"] == 2 and mesh.shape["sec"] == 4
    return jax.shard_map(
        shards_line if line else shards_any,
        mesh=mesh,
        in_specs=placed,
        out_specs=(P("sec", "col", None), P("sec", ("row", "col"), None)),
        check_vma=False,
    )
```

time: 605 us -> 354 us (0.59)
  waiting for transfers between devices: 409 us -> 197 us
  matrix products: 162 us -> 0 us
  Pallas kernels: 0 us -> 83.5 us
  starting transfers between devices: 0.72 us -> 63.9 us
  between operations: 14.2 us -> 1.51 us
  local copies, waits for them, and re-layouts: 11.2 us -> 2.26 us
    ppermute x0 -> x46, waiting for transfers between devices: none -> 197 us  [the longest x6 140 us: hop(): lax.ppermute(value, AXES, [(a * n + c, b * n + c) for a, b in pairs for c...]
    psum x1 -> x0, waiting for transfers between devices: 168 us -> none  [run_segment(): child_sum = lax.psum(jnp.where(parent_flag, 0.0, update), ('sec', 'col'))]
    dot_general x4 -> x0, matrix products: 162 us -> none  [the longest x2 88.6 us: run_segment(): jnp.dot(masked, solved, precision=highest, preferred_element_type=jnp.flo...]
    reduce_scatter x4 -> x0, waiting for transfers between devices: 133 us -> none  [the longest x2 112 us: run_segment(): shares = lax.psum_scatter(update, 'col', scatter_dimension=0, tiled=True)]
    all_gather x3 -> x0, waiting for transfers between devices: 107 us -> none  [the longest x1 81.1 us: shards(): rows_full = lax.all_gather(rhs[0], 'col', axis=0, tiled=True)]
    pallas_call x0 -> x16, Pallas kernels: none -> 83.5 us  [the longest x8 41.5 us: factor_pieces(): pl.pallas_call(functools.partial(pieces_body, role, pieces_at, counts, st...]
    ppermute x0 -> x46, starting transfers between devices: none -> 63.9 us  [the longest x36 55.5 us: send(): lax.ppermute(value, AXES, [(s * n + a, s * n + b) for s in secs for a, b...]
    mul x1 -> x0, local copies, waits for them, and re-layouts: 11.1 us -> none  [shards(): coupling_local.reshape(occupancy.shape[0], block_rows, occupancy.shape[1]...]
  transfers between devices with their start and end apart: 8 -> 46, of which waited for: 8 -> 17; matrix products, arithmetic and copies ran while one was open for 8% -> 1% of each run, Pallas kernels for 0% -> 19%
where the time goes in v1:
time: 354 us; the launch traced here: 353 us
  waiting for transfers between devices  197 us (56%)
  Pallas kernels  83.5 us (24%)
  starting transfers between devices  63.9 us (18%)
  other arithmetic  4.51 us (1%)
    ppermute x6, waiting for transfers between devices, hop(): lax.ppermute(value, AXES, [(a * n + c, b * n + c) for a, b in pairs for c...  140 us
    ppermute x36, starting transfers between devices, send(): lax.ppermute(value, AXES, [(s * n + a, s * n + b) for s in secs for a, b...  55.5 us
    ppermute x36, waiting for transfers between devices, send(): lax.ppermute(value, AXES, [(s * n + a, s * n + b) for s in secs for a, b...  54.3 us
    pallas_call x8, Pallas kernels, factor_pieces(): pl.pallas_call(functools.partial(pieces_body, role, pieces_at, counts, st...  41.5 us
    pallas_call x4, Pallas kernels, panel_rest(): pl.pallas_call(functools.partial(rest_body, role), out_shape=tuple((jax.S...  28.3 us
    pallas_call x4, Pallas kernels, panel_first(): pl.pallas_call(functools.partial(first_body, role), out_shape=(jax.ShapeD...  13.7 us
    ppermute x6, starting transfers between devices, hop(): lax.ppermute(value, AXES, [(a * n + c, b * n + c) for a, b in pairs for c...  7.88 us
  transfers between devices with their start and end apart: 46, of which 17 were waited for; matrix products, arithmetic and copies ran while one was open for 1% of the time, Pallas kernels for 19%

profile of v1, /device:TPU:14, one launch (start us, length us, event | category | flops | bytes accessed | tf_op | source)
XLA Modules:
  0.0 352.7 jit_solution(11701570161715586611)
XLA Ops:
  25.9 126.1 %collective-permute-done.17 = f32[1024,128]{1,0:T(8,128)S(1)} collective-permute-done((f32[1024,128]{1,0:T(8,128)S(1)}, f32[1024,128]{1,0:T(8,128)S(1)}, u32[]{:S(2)}, u32[]{:S(2)}) %collective-permute-start.17) | collective-permute-done | bytes 524320 | tf_op jit(solution)/shard_map/ppermute | solution.py:315
  152.0 11.9 %collective-permute-done.16 = f32[1024,128]{1,0:T(8,128)S(1)} collective-permute-done((f32[1024,128]{1,0:T(8,128)S(1)}, f32[1024,128]{1,0:T(8,128)S(1)}, u32[]{:S(2)}, u32[]{:S(2)}) %collective-permute-start.16) | collective-permute-done | bytes 524320 | tf_op jit(solution)/shard_map/ppermute | solution.py:315
  167.5 3.0 collective-permute-start.18
  172.0 8.7 %collective-permute-done.19.refs_1_ = f32[1024,128]{1,0:T(8,128)S(1)} collective-permute-done((f32[1024,128]{1,0:T(8,128)S(1)}, f32[1024,128]{1,0:T(8,128)S(1)}, u32[]{:S(2)}, u32[]{:S(2)}) %collective-permute-start.19) | collective-permute-done | bytes 524320 | tf_op jit(solution)/shard_map/ppermute | solution.py:310
  182.6 2.9 collective-permute-start.29
  190.9 5.9 %collective-permute-done.29.refs_0_ = f32[1024,128]{1,0:T(8,128)S(1)} collective-permute-done((f32[1024,128]{1,0:T(8,128)S(1)}, f32[1024,128]{1,0:T(8,128)S(1)}, u32[]{:S(2)}, u32[]{:S(2)}) %collective-permute-start.29) | collective-permute-done | bytes 524320 | tf_op jit(solution)/shard_map/ppermute | solution.py:310
  196.8 4.3 %collective-permute-start.30 = (f32[1024,128]{1,0:T(8,128)S(1)}, f32[1024,128]{1,0:T(8,128)S(1)}, u32[]{:S(2)}, u32[]{:S(2)}) collective-permute-start(f32[1024,128]{1,0:T(8,128)S(1)} %collective-permute-done.29.refs_0_), channel_id=1, source_target_pairs={{25,24},{26,27},{29,28},{30,31}} | collective-permute-start | bytes 1572872 | tf_op jit(solution)/shard_map/ppermute | solution.py:310
  201.1 12.2 %shard_map.76.refs_2_ = f32[2048,128]{1,0:T(8,128)S(1)} custom-call(s32[11]{0:T(128)S(1)} %pad_add_fusion.meta, f32[2048,4096]{1,0:T(8,128)} %bitcast.30, f32[1024,128]{1,0:T(8,128)S(1)} %slice_subtract_fusion, f32[1024,128]{1,0:T(8,128)S(1)} %collective-permute-done.19.refs_1_, f32[1024,128]{1,0:T(8,128)S(1)} %collective-permute-done.18.refs_2_, ...), custom_call_target="tpu_custom_call" | custom-call | flops 1 | bytes 1 | tf_op jit(solution)/shard_map/pallas_call | solution.py:117
  215.8 7.0 %shard_map.77.mine_ref = f32[2048,128]{1,0:T(8,128)S(1)} custom-call(s32[11]{0:T(128)S(1)} %pad_add_fusion.meta, f32[2048,4096]{1,0:T(8,128)} %bitcast.31, f32[1024,128]{1,0:T(8,128)S(1)} %collective-permute-done.29.refs_0_, f32[1024,128]{1,0:T(8,128)S(1)} %collective-permute-done.30.refs_1_, f32[2048,128]{1,0:T(8,128)S(1)} %shard_map.76.refs_2_), custom_call_target="tpu_custom_call" | custom-call | flops 1 | bytes 1 | tf_op jit(solution)/shard_map/pallas_call | solution.py:117
  227.7 6.2 %shard_map.78 = (f32[2048,128]{1,0:T(8,128)S(1)}, bf16[2048,256]{1,0:T(8,128)(2,1)S(1)}, f32[1024,128]{1,0:T(8,128)S(1)}) custom-call(s32[11]{0:T(128)S(1)} %pad_add_fusion.meta, f32[4096,2048]{1,0:T(8,128)} %bitcast.38, f32[32,2048]{1,0:T(8,128)S(1)} %bitcast.22, f32[2048,128]{1,0:T(8,128)S(1)} %shard_map.77.mine_ref, ...), custom_call_target="tpu_custom_call" | custom-call | flops 1 | bytes 1 | tf_op jit(solution)/shard_map/pallas_call | solution.py:205
  233.9 5.2 %collective-permute-done.33.refs_1_ = f32[1024,128]{1,0:T(8,128)S(1)} collective-permute-done((f32[1024,128]{1,0:T(8,128)S(1)}, f32[1024,128]{1,0:T(8,128)S(1)}, u32[]{:S(2)}, u32[]{:S(2)}) %collective-permute-start.33) | collective-permute-done | bytes 524320 | tf_op jit(solution)/shard_map/ppermute | solution.py:310
  243.0 2.9 collective-permute-start.34
  245.9 13.4 %shard_map.79 = (f32[1024,128]{1,0:T(8,128)S(1)}, f32[1024,128]{1,0:T(8,128)S(1)}, f32[1024,128]{1,0:T(8,128)S(1)}) custom-call(s32[11]{0:T(128)S(1)} %pad_add_fusion.meta, f32[4096,2048]{1,0:T(8,128)} %bitcast.39, f32[32,2048]{1,0:T(8,128)S(1)} %bitcast.23, bf16[2048,256]{1,0:T(8,128)(2,1)S(1)} %get-tuple-element.180.words_ref), custom_call_target="tpu_custom_call" | custom-call | flops 1 | bytes 1 | tf_op jit(solution)/shard_map/pallas_call | solution.py:289
  261.3 2.9 collective-permute-start.36
  264.3 12.2 %shard_map.80.refs_2_ = f32[2048,128]{1,0:T(8,128)S(1)} custom-call(s32[11]{0:T(128)S(1)} %pad_add_fusion.meta, f32[2048,4096]{1,0:T(8,128)} %bitcast.32, f32[1024,128]{1,0:T(8,128)S(1)} %add_subtract_fusion.refs_0_, f32[1024,128]{1,0:T(8,128)S(1)} %collective-permute-done.33.refs_1_, f32[1024,128]{1,0:T(8,128)S(1)} %collective-permute-done.32.refs_2_, ...), custom_call_target="tpu_custom_call" | custom-call | flops 1 | bytes 1 | tf_op jit(solution)/shard_map/pallas_call | solution.py:117
  276.5 7.3 %shard_map.81.mine_ref = f32[2048,128]{1,0:T(8,128)S(1)} custom-call(s32[11]{0:T(128)S(1)} %pad_add_fusion.meta, f32[2048,4096]{1,0:T(8,128)} %bitcast.33, f32[1024,128]{1,0:T(8,128)S(1)} %collective-permute-done.34.refs_0_, f32[1024,128]{1,0:T(8,128)S(1)} %collective-permute-done.37.refs_1_, f32[2048,128]{1,0:T(8,128)S(1)} %shard_map.80.refs_2_), custom_call_target="tpu_custom_call" | custom-call | flops 1 | bytes 1 | tf_op jit(solution)/shard_map/pallas_call | solution.py:117
  285.9 2.9 collective-permute-start.40
  288.8 6.2 %shard_map.82 = (f32[2048,128]{1,0:T(8,128)S(1)}, bf16[2048,256]{1,0:T(8,128)(2,1)S(1)}, f32[1024,128]{1,0:T(8,128)S(1)}) custom-call(s32[11]{0:T(128)S(1)} %pad_add_fusion.meta, f32[4096,2048]{1,0:T(8,128)} %bitcast.40, f32[32,2048]{1,0:T(8,128)S(1)} %bitcast.24, f32[2048,128]{1,0:T(8,128)S(1)} %shard_map.81.mine_ref, ...), custom_call_target="tpu_custom_call" | custom-call | flops 1 | bytes 1 | tf_op jit(solution)/shard_map/pallas_call | solution.py:205
  295.0 5.1 %collective-permute-done.39 = f32[1024,128]{1,0:T(8,128)S(1)} collective-permute-done((f32[1024,128]{1,0:T(8,128)S(1)}, f32[1024,128]{1,0:T(8,128)S(1)}, u32[]{:S(2)}, u32[]{:S(2)}) %collective-permute-start.39) | collective-permute-done | bytes 524320 | tf_op jit(solution)/shard_map/ppermute | solution.py:310
  303.4 13.4 %shard_map.83 = (f32[1024,128]{1,0:T(8,128)S(1)}, f32[1024,128]{1,0:T(8,128)S(1)}, f32[1024,128]{1,0:T(8,128)S(1)}) custom-call(s32[11]{0:T(128)S(1)} %pad_add_fusion.meta, f32[4096,2048]{1,0:T(8,128)} %bitcast.41, f32[32,2048]{1,0:T(8,128)S(1)} %bitcast.25, bf16[2048,256]{1,0:T(8,128)(2,1)S(1)} %get-tuple-element.206.words_ref), custom_call_target="tpu_custom_call" | custom-call | flops 1 | bytes 1 | tf_op jit(solution)/shard_map/pallas_call | solution.py:289
  317.6 2.9 collective-permute-start.42
  321.9 10.5 %collective-permute-done.42 = f32[1024,128]{1,0:T(8,128)S(1)} collective-permute-done((f32[1024,128]{1,0:T(8,128)S(1)}, f32[1024,128]{1,0:T(8,128)S(1)}, u32[]{:S(2)}, u32[]{:S(2)}) %collective-permute-start.42) | collective-permute-done | bytes 524320 | tf_op jit(solution)/shard_map/ppermute | solution.py:310
  335.2 2.9 collective-permute-start.45
  341.7 7.2 %collective-permute-done.45 = f32[1024,128]{1,0:T(8,128)S(1)} collective-permute-done((f32[1024,128]{1,0:T(8,128)S(1)}, f32[1024,128]{1,0:T(8,128)S(1)}, u32[]{:S(2)}, u32[]{:S(2)}) %collective-permute-start.45) | collective-permute-done | bytes 524320 | tf_op jit(solution)/shard_map/ppermute | solution.py:310
  (122 shorter events, 68.1 us)
Async XLA Ops:
  20.3 131.8 %collective-permute-start.17 = (f32[1024,128]{1,0:T(8,128)S(1)}, f32[1024,128]{1,0:T(8,128)S(1)}, u32[]{:S(2)}, u32[]{:S(2)}) collective-permute-start(f32[1024,128]{1,0:T(8,128)S(1)} %add_add_fusion.3), channel_id=1, source_target_pairs={{16,24},{17,25},{18,26},{19,27},{20,28},{21,29},{22,30},{23,31}} | collective-permute-start | bytes 1572872 | tf_op jit(solution)/shard_map/ppermute | solution.py:315
  21.7 142.3 %collective-permute-start.16 = (f32[1024,128]{1,0:T(8,128)S(1)}, f32[1024,128]{1,0:T(8,128)S(1)}, u32[]{:S(2)}, u32[]{:S(2)}) collective-permute-start(f32[1024,128]{1,0:T(8,128)S(1)} %add_add_fusion.3), channel_id=1, source_target_pairs={{8,24},{9,25},{10,26},{11,27},{12,28},{13,29},{14,30},{15,31}} | collective-permute-start | bytes 1572872 | tf_op jit(solution)/shard_map/ppermute | solution.py:315
  23.0 141.0 %collective-permute-start.15 = (f32[1024,128]{1,0:T(8,128)S(1)}, f32[1024,128]{1,0:T(8,128)S(1)}, u32[]{:S(2)}, u32[]{:S(2)}) collective-permute-start(f32[1024,128]{1,0:T(8,128)S(1)} %add_add_fusion.3), channel_id=1, source_target_pairs={{0,24},{1,25},{2,26},{3,27},{4,28},{5,29},{6,30},{7,31}} | collective-permute-start | bytes 1572872 | tf_op jit(solution)/shard_map/ppermute | solution.py:315
  24.3 139.8 %collective-permute-start.20 = (f32[1024,128]{1,0:T(8,128)S(1)}, f32[1024,128]{1,0:T(8,128)S(1)}, u32[]{:S(2)}, u32[]{:S(2)}) collective-permute-start(f32[1024,128]{1,0:T(8,128)S(1)} %get-tuple-element.159), channel_id=1, source_target_pairs={{0,1},{3,2},{8,9},{11,10},{16,17},{19,18},{4,5},{7,6},{12,13},{15,... | collective-permute-start | bytes 1572872 | tf_op jit(solution)/shard_map/ppermute | solution.py:310
  165.6 15.1 %collective-permute-start.19 = (f32[1024,128]{1,0:T(8,128)S(1)}, f32[1024,128]{1,0:T(8,128)S(1)}, u32[]{:S(2)}, u32[]{:S(2)}) collective-permute-start(f32[1024,128]{1,0:T(8,128)S(1)} %slice_subtract_fusion), channel_id=1, source_target_pairs={{24,25},{25,24},{26,27},{27,26},{28,29},{29,28},{30,31},{31,30}} | collective-permute-start | bytes 1572872 | tf_op jit(solution)/shard_map/ppermute | solution.py:310
  167.5 15.1 %collective-permute-start.18 = (f32[1024,128]{1,0:T(8,128)S(1)}, f32[1024,128]{1,0:T(8,128)S(1)}, u32[]{:S(2)}, u32[]{:S(2)}) collective-permute-start(f32[1024,128]{1,0:T(8,128)S(1)} %slice_subtract_fusion), channel_id=1, source_target_pairs={{25,26},{26,25},{29,30},{30,29}} | collective-permute-start | bytes 1572872 | tf_op jit(solution)/shard_map/ppermute | solution.py:310
  170.6 16.3 %collective-permute-start.24 = (f32[1024,128]{1,0:T(8,128)S(1)}, f32[1024,128]{1,0:T(8,128)S(1)}, u32[]{:S(2)}, u32[]{:S(2)}) collective-permute-start(f32[1024,128]{1,0:T(8,128)S(1)} %add.86), channel_id=1, source_target_pairs={{1,2},{2,1},{9,10},{10,9},{17,18},{18,17},{5,6},{6,5},{13,14},{14,... | collective-permute-start | bytes 1572872 | tf_op jit(solution)/shard_map/ppermute | solution.py:310
  171.3 15.6 %collective-permute-start.23 = (f32[1024,128]{1,0:T(8,128)S(1)}, f32[1024,128]{1,0:T(8,128)S(1)}, u32[]{:S(2)}, u32[]{:S(2)}) collective-permute-start(f32[1024,128]{1,0:T(8,128)S(1)} %add.84), channel_id=1, source_target_pairs={{0,1},{1,0},{2,3},{3,2},{8,9},{9,8},{10,11},{11,10},{16,17},{17,16... | collective-permute-start | bytes 1572872 | tf_op jit(solution)/shard_map/ppermute | solution.py:310
  182.6 14.2 %collective-permute-start.29 = (f32[1024,128]{1,0:T(8,128)S(1)}, f32[1024,128]{1,0:T(8,128)S(1)}, u32[]{:S(2)}, u32[]{:S(2)}) collective-permute-start(f32[1024,128]{1,0:T(8,128)S(1)} %collective-permute-done.19.refs_1_), channel_id=1, source_target_pairs={{25,26},{26,25},{29,30},{30,29}} | collective-permute-start | bytes 1572872 | tf_op jit(solution)/shard_map/ppermute | solution.py:310
  187.0 26.3 %collective-permute-start.27 = (f32[1024,128]{1,0:T(8,128)S(1)}, f32[1024,128]{1,0:T(8,128)S(1)}, u32[]{:S(2)}, u32[]{:S(2)}) collective-permute-start(f32[1024,128]{1,0:T(8,128)S(1)} %add_add_fusion.1), channel_id=1, source_target_pairs={{16,24},{17,25},{18,26},{19,27},{20,28},{21,29},{22,30},{23,31}} | collective-permute-start | bytes 1572872 | tf_op jit(solution)/shard_map/ppermute | solution.py:315
  188.3 27.3 %collective-permute-start.26 = (f32[1024,128]{1,0:T(8,128)S(1)}, f32[1024,128]{1,0:T(8,128)S(1)}, u32[]{:S(2)}, u32[]{:S(2)}) collective-permute-start(f32[1024,128]{1,0:T(8,128)S(1)} %add_add_fusion.1), channel_id=1, source_target_pairs={{8,24},{9,25},{10,26},{11,27},{12,28},{13,29},{14,30},{15,31}} | collective-permute-start | bytes 1572872 | tf_op jit(solution)/shard_map/ppermute | solution.py:315
  189.6 26.0 %collective-permute-start.25 = (f32[1024,128]{1,0:T(8,128)S(1)}, f32[1024,128]{1,0:T(8,128)S(1)}, u32[]{:S(2)}, u32[]{:S(2)}) collective-permute-start(f32[1024,128]{1,0:T(8,128)S(1)} %add_add_fusion.1), channel_id=1, source_target_pairs={{0,24},{1,25},{2,26},{3,27},{4,28},{5,29},{6,30},{7,31}} | collective-permute-start | bytes 1572872 | tf_op jit(solution)/shard_map/ppermute | solution.py:315
  196.8 19.0 %collective-permute-start.30 = (f32[1024,128]{1,0:T(8,128)S(1)}, f32[1024,128]{1,0:T(8,128)S(1)}, u32[]{:S(2)}, u32[]{:S(2)}) collective-permute-start(f32[1024,128]{1,0:T(8,128)S(1)} %collective-permute-done.29.refs_0_), channel_id=1, source_target_pairs={{25,24},{26,27},{29,28},{30,31}} | collective-permute-start | bytes 1572872 | tf_op jit(solution)/shard_map/ppermute | solution.py:310
  222.9 16.2 %collective-permute-start.33 = (f32[1024,128]{1,0:T(8,128)S(1)}, f32[1024,128]{1,0:T(8,128)S(1)}, u32[]{:S(2)}, u32[]{:S(2)}) collective-permute-start(f32[1024,128]{1,0:T(8,128)S(1)} %add_subtract_fusion.refs_0_), channel_id=1, source_target_pairs={{24,25},{25,24},{26,27},{27,26},{28,29},{29,28},{30,31},{31,30}} | collective-permute-start | bytes 1572872 | tf_op jit(solution)/shard_map/ppermute | solution.py:310
  224.8 16.2 %collective-permute-start.32 = (f32[1024,128]{1,0:T(8,128)S(1)}, f32[1024,128]{1,0:T(8,128)S(1)}, u32[]{:S(2)}, u32[]{:S(2)}) collective-permute-start(f32[1024,128]{1,0:T(8,128)S(1)} %add_subtract_fusion.refs_0_), channel_id=1, source_target_pairs={{25,26},{26,25},{29,30},{30,29}} | collective-permute-start | bytes 1572872 | tf_op jit(solution)/shard_map/ppermute | solution.py:310
  241.1 18.2 %collective-permute-start.35 = (f32[1024,128]{1,0:T(8,128)S(1)}, f32[1024,128]{1,0:T(8,128)S(1)}, u32[]{:S(2)}, u32[]{:S(2)}) collective-permute-start(f32[1024,128]{1,0:T(8,128)S(1)} %broadcast_select_fusion.4), channel_id=1, source_target_pairs={{24,25},{25,24},{26,27},{27,26},{28,29},{29,28},{30,31},{31,30}} | collective-permute-start | bytes 1572872 | tf_op jit(solution)/shard_map/ppermute | solution.py:310
  243.0 16.3 %collective-permute-start.34 = (f32[1024,128]{1,0:T(8,128)S(1)}, f32[1024,128]{1,0:T(8,128)S(1)}, u32[]{:S(2)}, u32[]{:S(2)}) collective-permute-start(f32[1024,128]{1,0:T(8,128)S(1)} %collective-permute-done.33.refs_1_), channel_id=1, source_target_pairs={{25,26},{26,25},{29,30},{30,29}} | collective-permute-start | bytes 1572872 | tf_op jit(solution)/shard_map/ppermute | solution.py:310
  259.3 17.1 %collective-permute-start.37 = (f32[1024,128]{1,0:T(8,128)S(1)}, f32[1024,128]{1,0:T(8,128)S(1)}, u32[]{:S(2)}, u32[]{:S(2)}) collective-permute-start(f32[1024,128]{1,0:T(8,128)S(1)} %broadcast_select_fusion.3), channel_id=1, source_target_pairs={{24,25},{25,24},{26,27},{27,26},{28,29},{29,28},{30,31},{31,30}} | collective-permute-start | bytes 1572872 | tf_op jit(solution)/shard_map/ppermute | solution.py:310
  261.3 15.1 %collective-permute-start.36 = (f32[1024,128]{1,0:T(8,128)S(1)}, f32[1024,128]{1,0:T(8,128)S(1)}, u32[]{:S(2)}, u32[]{:S(2)}) collective-permute-start(f32[1024,128]{1,0:T(8,128)S(1)} %add.90), channel_id=1, source_target_pairs={{25,26},{26,25},{29,30},{30,29}} | collective-permute-start | bytes 1572872 | tf_op jit(solution)/shard_map/ppermute | solution.py:310
  284.0 16.2 %collective-permute-start.39 = (f32[1024,128]{1,0:T(8,128)S(1)}, f32[1024,128]{1,0:T(8,128)S(1)}, u32[]{:S(2)}, u32[]{:S(2)}) collective-permute-start(f32[1024,128]{1,0:T(8,128)S(1)} %add.91), channel_id=1, source_target_pairs={{24,25},{25,24},{26,27},{27,26},{28,29},{29,28},{30,31},{31,30}} | collective-permute-start | bytes 1572872 | tf_op jit(solution)/shard_map/ppermute | solution.py:310
  285.9 16.2 %collective-permute-start.40 = (f32[1024,128]{1,0:T(8,128)S(1)}, f32[1024,128]{1,0:T(8,128)S(1)}, u32[]{:S(2)}, u32[]{:S(2)}) collective-permute-start(f32[1024,128]{1,0:T(8,128)S(1)} %add.92), channel_id=1, source_target_pairs={{25,26},{26,25},{29,30},{30,29}} | collective-permute-start | bytes 1572872 | tf_op jit(solution)/shard_map/ppermute | solution.py:310
  302.1 15.4 %collective-permute-start.41 = (f32[1024,128]{1,0:T(8,128)S(1)}, f32[1024,128]{1,0:T(8,128)S(1)}, u32[]{:S(2)}, u32[]{:S(2)}) collective-permute-start(f32[1024,128]{1,0:T(8,128)S(1)} %get-tuple-element.211), channel_id=1, source_target_pairs={{24,25},{27,26},{28,29},{31,30}} | collective-permute-start | bytes 1572872 | tf_op jit(solution)/shard_map/ppermute | solution.py:310
  317.6 14.9 %collective-permute-start.42 = (f32[1024,128]{1,0:T(8,128)S(1)}, f32[1024,128]{1,0:T(8,128)S(1)}, u32[]{:S(2)}, u32[]{:S(2)}) collective-permute-start(f32[1024,128]{1,0:T(8,128)S(1)} %add.95), channel_id=1, source_target_pairs={{25,26},{26,25},{29,30},{30,29}} | collective-permute-start | bytes 1572872 | tf_op jit(solution)/shard_map/ppermute | solution.py:310
  320.5 14.6 %collective-permute-start.43 = (f32[1024,128]{1,0:T(8,128)S(1)}, f32[1024,128]{1,0:T(8,128)S(1)}, u32[]{:S(2)}, u32[]{:S(2)}) collective-permute-start(f32[1024,128]{1,0:T(8,128)S(1)} %get-tuple-element.216), channel_id=1, source_target_pairs={{24,25},{27,26},{28,29},{31,30}} | collective-permute-start | bytes 1572872 | tf_op jit(solution)/shard_map/ppermute | solution.py:310
  (24 other events, 238.8 us)

commit v2 on v1

--- a/solution.py
+++ b/solution.py
@@ -134,6 +134,65 @@
     )(meta, factor, *flat)
 
 
+def last_body(role, meta, block_ref, inner_ref, end_ref, total_ref, out_ref, held, words, sums, in_sem, out_sem):
+    width = held.shape[1]
+    tiles = out_sem.shape[0]
+    tile = block_ref.shape[0] // tiles
+
+    @pl.when(meta[role] == 1)
+    def _():
+        def out_copy(t):
+            rows = pl.ds(pl.multiple_of(t * tile, tile), tile)
+            return pltpu.make_async_copy(sums.at[rows], out_ref.at[rows], out_sem.at[t])
+
+        @pl.when(meta[AT_END] == 0)
+        def _():
+            pltpu.make_async_copy(inner_ref, held, in_sem.at[0]).start()
+
+        @pl.when(meta[AT_END] == 1)
+        def _():
+            pltpu.make_async_copy(end_ref, held, in_sem.at[0]).start()
+
+        sum_copy = pltpu.make_async_copy(total_ref, sums, in_sem.at[1])
+        sum_copy.start()
+        pltpu.make_async_copy(end_ref, held, in_sem.at[0]).wait()
+        high, low = split_words(held[...])
+        words[:, :width] = high
+        words[:, width:] = low
+        sum_copy.wait()
+
+        @pl.loop(0, tiles)
+        def _(t):
+            rows = pl.ds(pl.multiple_of(t * tile, tile), tile)
+            sums[rows, :] = three_term(block_ref[rows, :], words[...], width) + sums[rows, :]
+            out_copy(t).start()
+
+        for t in range(tiles):
+            out_copy(t).wait()
+
+
+def last_piece(role, meta, block, inner, end, total):
+    rows, depth = block.shape
+    width = inner.shape[1]
+    tiles = rows // min(rows, 512)
+    anywhere = pl.BlockSpec(memory_space=pl.ANY)
+    return pl.pallas_call(
+        functools.partial(last_body, role),
+        out_shape=jax.ShapeDtypeStruct((rows, width), F32),
+        in_specs=[pl.BlockSpec(memory_space=pltpu.SMEM), pl.BlockSpec(memory_space=pltpu.VMEM)] + [anywhere] * 3,
+        out_specs=anywhere,
+        scratch_shapes=[
+            pltpu.VMEM((depth, width), F32),
+            pltpu.VMEM((depth, 2 * width), BF16),
+            pltpu.VMEM((rows, width), F32),
+            pltpu.SemaphoreType.DMA((2,)),
+            pltpu.SemaphoreType.DMA((tiles,)),
+        ],
+        compiler_params=pltpu.CompilerParams(vmem_limit_bytes=VMEM_LIMIT),
+        cost_estimate=COST,
+    )(meta, block, inner, end, total)
+
+
 def masked_terms(panel, mask_ref, words, base, block_rows, width):
     parts = []
     for j in range(panel.shape[0] // block_rows):
@@ -143,20 +202,15 @@
 
 
 def first_body(
-    role, meta, panel_ref, mask_ref, mine_ref, other_ref, solved_ref, words_ref, out_ref,
-    panel, mask, held, words, sums, panel_sem, in_sem, solved_sem, words_sem, out_sem,
+    role, meta, block_ref, mine_ref, other_ref, solved_ref, words_ref, out_ref,
+    held, words, sums, in_sem, solved_sem, words_sem, out_sem,
 ):
-    tiles, tile, depth = panel.shape
     width = held.shape[2]
-    block_rows = panel_ref.shape[0] // mask_ref.shape[0]
-    per = tile // block_rows
+    tiles = out_sem.shape[0]
+    tile = block_ref.shape[0] // tiles
 
     @pl.when(meta[role] == 1)
     def _():
-        def tile_copy(t):
-            rows = pl.ds(pl.multiple_of((meta[SHARD] * tiles + t) * tile, tile), tile)
-            return pltpu.make_async_copy(panel_ref.at[rows], panel.at[t], panel_sem.at[t])
-
         def out_copy(t):
             rows = pl.ds(pl.multiple_of(t * tile, tile), tile)
             return pltpu.make_async_copy(sums.at[rows], out_ref.at[rows], out_sem.at[t])
@@ -164,12 +218,9 @@
         inputs = [
             pltpu.make_async_copy(mine_ref, held.at[0], in_sem.at[0]),
             pltpu.make_async_copy(other_ref, held.at[1], in_sem.at[1]),
-            pltpu.make_async_copy(mask_ref, mask, in_sem.at[2]),
         ]
         for copy in inputs:
             copy.start()
-        for t in range(tiles):
-            tile_copy(t).start()
         for copy in inputs:
             copy.wait()
         solved = held[0] + held[1]
@@ -179,28 +230,25 @@
         words[:, width:] = low
         solved_copy = pltpu.make_async_copy(held.at[0], solved_ref, solved_sem)
         words_copy = pltpu.make_async_copy(words, words_ref, words_sem)
+        solved_copy.start()
+        words_copy.start()
 
         @pl.loop(0, tiles)
         def _(t):
-            tile_copy(t).wait()
-            parts = masked_terms(panel[t], mask, words[...], (meta[SHARD] * tiles + t) * per, block_rows, width)
-            for j, part in enumerate(parts):
-                sums[pl.ds(pl.multiple_of(t * tile + j * block_rows, block_rows), block_rows), :] = part
+            rows = pl.ds(pl.multiple_of(t * tile, tile), tile)
+            sums[rows, :] = three_term(block_ref[rows, :], words[...], width)
             out_copy(t).start()
 
-        solved_copy.start()
-        words_copy.start()
         for t in range(tiles):
             out_copy(t).wait()
         solved_copy.wait()
         words_copy.wait()
 
 
-def panel_first(role, meta, n, panel, mask, mine, other):
+def panel_first(role, meta, block, mine, other):
     depth, width = mine.shape
-    rows = panel.shape[0] // n
-    tile = min(rows, 256)
-    tiles = rows // tile
+    rows = block.shape[0]
+    tiles = rows // min(rows, 256)
     anywhere = pl.BlockSpec(memory_space=pl.ANY)
     return pl.pallas_call(
         functools.partial(first_body, role),
@@ -209,26 +257,69 @@
             jax.ShapeDtypeStruct((depth, 2 * width), BF16),
             jax.ShapeDtypeStruct((rows, width), F32),
         ),
-        in_specs=[pl.BlockSpec(memory_space=pltpu.SMEM)] + [anywhere] * 4,
+        in_specs=[pl.BlockSpec(memory_space=pltpu.SMEM), pl.BlockSpec(memory_space=pltpu.VMEM)] + [anywhere] * 2,
         out_specs=(anywhere,) * 3,
         scratch_shapes=[
-            pltpu.VMEM((tiles, tile, depth), F32),
-            pltpu.VMEM(mask.shape, F32),
             pltpu.VMEM((2, depth, width), F32),
             pltpu.VMEM((depth, 2 * width), BF16),
             pltpu.VMEM((rows, width), F32),
-            pltpu.SemaphoreType.DMA((tiles,)),
-            pltpu.SemaphoreType.DMA((3,)),
+            pltpu.SemaphoreType.DMA((2,)),
             pltpu.SemaphoreType.DMA,
             pltpu.SemaphoreType.DMA,
             pltpu.SemaphoreType.DMA((tiles,)),
         ],
         compiler_params=pltpu.CompilerParams(vmem_limit_bytes=VMEM_LIMIT),
         cost_estimate=COST,
-    )(meta, panel, mask, mine, other)
-
-
-def rest_body(role, meta, panel_ref, mask_ref, words_ref, *refs):
+    )(meta, block, mine, other)
+
+
+def block_body(role, meta, block_ref, words_ref, out_ref, words, sums, in_sem, out_sem):
+    width = sums.shape[1]
+    tiles = out_sem.shape[0]
+    tile = block_ref.shape[0] // tiles
+
+    @pl.when(meta[role] == 1)
+    def _():
+        def out_copy(t):
+            rows = pl.ds(pl.multiple_of(t * tile, tile), tile)
+            return pltpu.make_async_copy(sums.at[rows], out_ref.at[rows], out_sem.at[t])
+
+        words_copy = pltpu.make_async_copy(words_ref, words, in_sem)
+        words_copy.start()
+        words_copy.wait()
+
+        @pl.loop(0, tiles)
+        def _(t):
+            rows = pl.ds(pl.multiple_of(t * tile, tile), tile)
+            sums[rows, :] = three_term(block_ref[rows, :], words[...], width)
+            out_copy(t).start()
+
+        for t in range(tiles):
+            out_copy(t).wait()
+
+
+def panel_block(role, meta, block, words):
+    depth, wide = words.shape
+    rows = block.shape[0]
+    tiles = rows // min(rows, 256)
+    anywhere = pl.BlockSpec(memory_space=pl.ANY)
+    return pl.pallas_call(
+        functools.partial(block_body, role),
+        out_shape=jax.ShapeDtypeStruct((rows, wide // 2), F32),
+        in_specs=[pl.BlockSpec(memory_space=pltpu.SMEM), pl.BlockSpec(memory_space=pltpu.VMEM), anywhere],
+        out_specs=anywhere,
+        scratch_shapes=[
+            pltpu.VMEM((depth, wide), BF16),
+            pltpu.VMEM((rows, wide // 2), F32),
+            pltpu.SemaphoreType.DMA,
+            pltpu.SemaphoreType.DMA((tiles,)),
+        ],
+        compiler_params=pltpu.CompilerParams(vmem_limit_bytes=VMEM_LIMIT),
+        cost_estimate=COST,
+    )(meta, block, words)
+
+
+def rest_body(role, ahead, meta, panel_ref, mask_ref, words_ref, *refs):
     n_out = len(refs) - 7
     outs = refs[:n_out]
     panel, mask, words, sums, panel_sem, in_sem, out_sem = refs[n_out:]
@@ -242,7 +333,7 @@
     @pl.when(meta[role] == 1)
     def _():
         def tile_copy(k, t):
-            at = pl.ds(pl.multiple_of((meta[SHARD + 1 + k] * tiles + t) * tile, tile), tile)
+            at = pl.ds(pl.multiple_of((meta[SHARD + ahead + k] * tiles + t) * tile, tile), tile)
             slot = (k * tiles + t) % slots
             return pltpu.make_async_copy(panel_ref.at[at], panel.at[slot], panel_sem.at[slot])
 
@@ -266,20 +357,20 @@
             def _(t):
                 tile_copy(k, t).wait()
                 slot = (k * tiles + t) % slots
-                parts = masked_terms(panel[slot], mask, words[...], (meta[SHARD + 1 + k] * tiles + t) * per, block_rows, width)
-                for j, part in enumerate(parts):
-                    sums[k, pl.ds(pl.multiple_of(t * tile + j * block_rows, block_rows), block_rows), :] = part
+                base = (meta[SHARD + ahead + k] * tiles + t) * per
+                for j, part in enumerate(masked_terms(panel[slot], mask, words[...], base, block_rows, width)):
+                    at = pl.multiple_of(t * tile + j * block_rows, block_rows)
+                    sums[k, pl.ds(at, block_rows), :] = part
                 out_copy(k, t).start()
-                ahead = k + slots // tiles
-                if ahead < n_out:
-                    tile_copy(ahead, t).start()
+                if k + slots // tiles < n_out:
+                    tile_copy(k + slots // tiles, t).start()
 
         for k in range(n_out):
             for t in range(tiles):
                 out_copy(k, t).wait()
 
 
-def panel_rest(role, meta, n, panel, mask, words):
+def panel_rest(role, meta, n, ahead, panel, mask, words):
     depth, wide = words.shape
     width = wide // 2
     rows = panel.shape[0] // n
@@ -287,18 +378,18 @@
     tiles = rows // tile
     anywhere = pl.BlockSpec(memory_space=pl.ANY)
     return pl.pallas_call(
-        functools.partial(rest_body, role),
-        out_shape=tuple(jax.ShapeDtypeStruct((rows, width), F32) for _ in range(n - 1)),
+        functools.partial(rest_body, role, ahead),
+        out_shape=tuple(jax.ShapeDtypeStruct((rows, width), F32) for _ in range(n - ahead)),
         in_specs=[pl.BlockSpec(memory_space=pltpu.SMEM)] + [anywhere] * 3,
-        out_specs=(anywhere,) * (n - 1),
+        out_specs=(anywhere,) * (n - ahead),
         scratch_shapes=[
             pltpu.VMEM((tiles, tile, depth), F32),
             pltpu.VMEM(mask.shape, F32),
             pltpu.VMEM((depth, wide), BF16),
-            pltpu.VMEM((n - 1, rows, width), F32),
+            pltpu.VMEM((n - ahead, rows, width), F32),
             pltpu.SemaphoreType.DMA((tiles,)),
             pltpu.SemaphoreType.DMA((2,)),
-            pltpu.SemaphoreType.DMA((n - 1, tiles)),
+            pltpu.SemaphoreType.DMA((n - ahead, tiles)),
         ],
         compiler_params=pltpu.CompilerParams(vmem_limit_bytes=VMEM_LIMIT),
         cost_estimate=COST,
@@ -338,9 +429,9 @@
 
 
 class Line:
-    def __init__(self, role, secs, meta, inner, factor, panel, mask):
+    def __init__(self, role, secs, meta, inner, factor, panel, mask, blocks):
         self.role, self.secs, self.meta, self.inner = role, secs, meta, inner
-        self.factor, self.panel, self.mask = factor, panel, mask
+        self.factor, self.panel, self.mask, self.blocks = factor, panel, mask, blocks
 
     def send(self, value, pairs):
         return send(value, self.secs, pairs)
@@ -351,31 +442,48 @@
     def swap(self, value):
         return lax.ppermute(value, "row", [(0, 1), (1, 0)])
 
+    def last(self, inner, end, total):
+        return last_piece(self.role, self.meta, self.blocks[0], inner, end, total)
+
     def first(self, mine, other):
-        return panel_first(self.role, self.meta, len(LEAVE), self.panel, self.mask, mine, other)
+        return panel_first(self.role, self.meta, self.blocks[1], mine, other)
 
     def rest(self, words):
-        return panel_rest(self.role, self.meta, len(LEAVE), self.panel, self.mask, words)
+        return panel_rest(self.role, self.meta, len(LEAVE), 2, self.panel, self.mask, words)
+
+    def second(self, words):
+        return panel_block(self.role, self.meta, self.blocks[2], words)
 
     def both(self, inner, end):
         return jnp.where(self.inner, inner, end)
 
-    def pair(self, own_a, own_b, passed):
+    def pair(self, own_a, raw_b, to_b, passed):
         order = Order()
         side_a, mid_a = order.note(self.send(own_a, EDGES), self.send(own_a, MIDDLE))
-        order.note(self.meta, self.mask)
-        mid_a, side_a, self.meta, self.mask = order.step(mid_a, side_a, self.meta, self.mask)
+        prepare = len(self.blocks) == 2
+        if prepare:
+            late, early = self.blocks
+            late = late(self.meta)
+            mid_a, side_a, self.meta, self.mask, late = order.step(mid_a, side_a, self.meta, self.mask, late)
+            self.blocks = order.note(late, early(self.meta, self.mask, 0), early(self.meta, self.mask, 1))
+        else:
+            mid_a, side_a, own_a = order.step(mid_a, side_a, own_a)
         near_a, across_a = order.note(self.send(mid_a, INWARD), self.send(side_a, MIDDLE))
-        own_a, side_a, mid_a, near_a, across_a = order.step(own_a, side_a, mid_a, near_a, across_a)
+        tot_a = None if prepare else order.note(self.solve((0, 1), [[own_a], [side_a]], None))
+        own_a, side_a, mid_a, near_a, across_a, raw_b = order.step(own_a, side_a, mid_a, near_a, across_a, raw_b)
         far_a = order.note(self.send(across_a, INWARD))
-        tot_a = order.note(self.solve((0, 1, 2), [[own_a], [side_a], [mid_a, near_a]], None))
-        own_b, tot_a, across_a, far_a = order.step(own_b(), tot_a, across_a, far_a)
+        if prepare:
+            tot_a = order.note(self.solve((0, 1, 2), [[own_a], [side_a], [mid_a, near_a]], None))
+        else:
+            tot_a = order.note(self.solve((2,), [[mid_a, near_a]], tot_a))
+        own_b, tot_a, across_a, far_a = order.step(to_b(raw_b), tot_a, across_a, far_a)
         side_b, mid_b = order.note(self.send(own_b, EDGES), self.send(own_b, MIDDLE))
-        tot_a = self.solve((3,), [[across_a, far_a]], tot_a)
+        tot_a = self.last(across_a, far_a, tot_a)
         solved_a, words_a, r0_a = order.note(*self.first(tot_a, self.swap(tot_a)))
         mid_b, side_b, r0_a, words_a = order.step(mid_b, side_b, r0_a, words_a)
         near_b, across_b = order.note(self.send(self.both(mid_b, r0_a), EDGES), self.send(side_b, MIDDLE))
-        r1_a, r2_a, rown_a = order.note(*self.rest(words_a))
+        r1_a = order.note(self.second(words_a))
+        r2_a, rown_a = order.note(*self.rest(words_a))
         across_b, r0_a, r1_a, near_b, own_b, side_b, mid_b = order.step(
             across_b, r0_a, r1_a, near_b, own_b, side_b, mid_b
         )
@@ -384,15 +492,16 @@
         tot_b = order.note(self.solve((0, 1, 2), [[own_b], [side_b], [mid_b, near_b]], None))
         r2_a, got_a, r1_a, far_b, tot_b, across_b = order.step(r2_a, got_a, r1_a, far_b, tot_b, across_b)
         rs_a, rm_a = order.note(self.send(r2_a + got_a, EDGES), self.send(r1_a + far_b, MIDDLE))
-        tot_b = self.solve((3,), [[across_b, far_b]], tot_b)
+        tot_b = self.last(across_b, far_b, tot_b)
         solved_b, words_b, r0_b = order.note(*self.first(tot_b, self.swap(tot_b)))
         r0_b, words_b, rown_a, rs_a, rm_a = order.step(r0_b, words_b, rown_a, rs_a, rm_a)
         sent_a = rown_a + rs_a + rm_a
         near = order.note(self.send(r0_b, OUTWARD))
-        passed_a = order.note(passed(sent_a))
-        r1_b, r2_b, rown_b = order.note(*self.rest(words_b))
-        r0_b, near, r1_b = order.step(r0_b, near, r1_b)
+        passed_a = passed(sent_a)
+        r1_b = order.note(self.second(words_b))
+        r0_b, near, r1_b, passed_a, words_b = order.step(r0_b, near, r1_b, passed_a, words_b)
         far, got = order.note(self.send(r1_b, OUTWARD), self.send(r0_b + near, MIDDLE))
+        r2_b, rown_b = order.note(*self.rest(words_b))
         r2_b, got, r1_b, far = order.step(r2_b, got, r1_b, far)
         rs_b, rm_b = self.send(r2_b + got, EDGES), self.send(r1_b + far, MIDDLE)
         sent_b = rown_b + rs_b + rm_b
@@ -400,11 +509,13 @@
 
 
 def to_last(sent):
-    top = lax.axis_size("sec") - 1
-    total = hop(sent, ((0, top),))
-    for s in range(1, top):
-        total = total + hop(sent, ((s, top),))
-    return total
+    half = sent.shape[0] // 2
+    upper, lower = sent[:half], sent[half:]
+    got_upper = hop(upper, ((0, 1), (2, 3)))
+    got_lower = hop(lower, ((0, 2), (1, 3)))
+    sum_upper = hop(upper + got_upper, ((1, 3),))
+    sum_lower = hop(lower + got_lower, ((2, 3),))
+    return jnp.concatenate([got_upper + sum_upper, got_lower + sum_lower], axis=0)
 
 
 def shards_line(rhs, inv_factor, coupling, pattern):
@@ -417,13 +528,27 @@
     flags = jnp.stack([~is_parent, is_parent, ~inner]).astype(jnp.int32)
     orders = jnp.asarray([a + b for a, b in zip(ARRIVE, LEAVE)], jnp.int32)
     meta = jnp.concatenate([flags, orders[col]])
-    kids = Line(0, tuple(range(top)), meta, inner, factor, panel, mask)
+
+    height = panel.shape[0] // len(LEAVE)
+    per = height * mask.shape[0] // panel.shape[0]
+
+    def late(meta):
+        depth = rhs.shape[1]
+        return lax.dynamic_slice(factor, (0, meta[ORDER + 3] * depth), (factor.shape[0], depth))
+
+    def early(meta, mask, k):
+        rows = lax.dynamic_slice(panel, (meta[SHARD + k] * height, 0), (height, panel.shape[1]))
+        cover = lax.dynamic_slice(mask, (meta[SHARD + k] * per, 0), (per, panel.shape[1]))
+        rows = rows.reshape(per, height // per, panel.shape[1]) * cover[:, None, :]
+        return rows.reshape(height, panel.shape[1])
+
+    kids = Line(0, tuple(range(top)), meta, inner, factor, panel, mask, (late, early))
     half = rhs.shape[2] // 2
     own = [rhs[0][:, :half], rhs[0][:, half:]]
-    solved0, sent0, solved1, sent1, passed0 = kids.pair(own[0], lambda: own[1], to_last)
-    head = Line(1, (top,), kids.meta, inner, factor, panel, kids.mask)
+    solved0, sent0, solved1, sent1, passed0 = kids.pair(own[0], own[1], lambda rows: rows, to_last)
+    head = Line(1, (top,), kids.meta, inner, factor, panel, kids.mask, kids.blocks)
     psolved0, psent0, psolved1, psent1, _ = head.pair(
-        own[0] - passed0, lambda: own[1] - to_last(sent1), lambda sent: sent
+        own[0] - passed0, sent1, lambda sent: own[1] - to_last(sent), lambda sent: sent
     )
     pick = lambda p, c: jnp.where(is_parent, p, c)
     solution = jnp.concatenate([pick(psolved0, solved0), pick(psolved1, solved1)], axis=1)

time: 354 us -> 340 us (0.960)
  waiting for transfers between devices: 197 us -> 161 us
  local copies, waits for them, and re-layouts: 2.26 us -> 13.2 us
  other arithmetic: 4.51 us -> 12.5 us
    ppermute x6 -> x8, waiting for transfers between devices: 140 us -> 110 us  [hop(): lax.ppermute(value, AXES, [(a * n + c, b * n + c) for a, b in pairs for c...]
    pallas_call x8 -> x5, Pallas kernels: 41.5 us -> 30.2 us  [factor_pieces(): pl.pallas_call(functools.partial(pieces_body, role, pieces_at, counts, st...]
    pallas_call x4 -> x12, Pallas kernels: 28.3 us -> 39.3 us  [the longest x4 20.9 us: panel_rest(): pl.pallas_call(functools.partial(rest_body, role, ahead), out_shape=tuple...]
    dynamic_slice x0 -> x3, local copies, waits for them, and re-layouts: none -> 9.05 us  [the longest x1 8.35 us: late(): lax.dynamic_slice(factor, (0, meta[ORDER + 3] * depth), (factor.shape[0],...]
    mul x0 -> x1, other arithmetic: none -> 7.1 us  [early(): rows = rows.reshape(per, height // per, panel.shape[1]) * cover[:, None, :]]
    ppermute x36, waiting for transfers between devices: 54.3 us -> 48.8 us  [send(): lax.ppermute(value, AXES, [(s * n + a, s * n + b) for s in secs for a, b...]
    ppermute x6 -> x8, starting transfers between devices: 7.88 us -> 10.5 us  [hop(): lax.ppermute(value, AXES, [(a * n + c, b * n + c) for a, b in pairs for c...]
  transfers between devices with their start and end apart: 46 -> 48, of which waited for: 17 -> 21; matrix products, arithmetic and copies ran while one was open for 1% -> 6% of each run, Pallas kernels for 19% -> 21%
where the time goes in v2:
time: 340 us; the launch traced here: 339 us
  waiting for transfers between devices  161 us (47%)
  Pallas kernels  80.4 us (24%)
  starting transfers between devices  66.6 us (20%)
  local copies, waits for them, and re-layouts  13.2 us (4%)
  other arithmetic  12.5 us (4%)
  between operations  4.85 us (1%)
    ppermute x8, waiting for transfers between devices, hop(): lax.ppermute(value, AXES, [(a * n + c, b * n + c) for a, b in pairs for c...  110 us
    ppermute x36, starting transfers between devices, send(): lax.ppermute(value, AXES, [(s * n + a, s * n + b) for s in secs for a, b...  55.7 us
    ppermute x36, waiting for transfers between devices, send(): lax.ppermute(value, AXES, [(s * n + a, s * n + b) for s in secs for a, b...  48.8 us
    pallas_call x5, Pallas kernels, factor_pieces(): pl.pallas_call(functools.partial(pieces_body, role, pieces_at, counts, st...  30.2 us
    pallas_call x4, Pallas kernels, panel_rest(): pl.pallas_call(functools.partial(rest_body, role, ahead), out_shape=tuple...  20.9 us
    pallas_call x4, Pallas kernels, panel_first(): pl.pallas_call(functools.partial(first_body, role), out_shape=(jax.ShapeD...  10.9 us
    ppermute x8, starting transfers between devices, hop(): lax.ppermute(value, AXES, [(a * n + c, b * n + c) for a, b in pairs for c...  10.5 us
    pallas_call x4, Pallas kernels, panel_block(): pl.pallas_call(functools.partial(block_body, role), out_shape=jax.ShapeDt...  9.66 us
  transfers between devices with their start and end apart: 48, of which 21 were waited for; matrix products, arithmetic and copies ran while one was open for 6% of the time, Pallas kernels for 21%

profile of v2, /device:TPU:14, one launch (start us, length us, event | category | flops | bytes accessed | tf_op | source)
XLA Modules:
  0.0 338.6 jit_solution(17913943454052537340)
XLA Ops:
  7.9 8.3 %dynamic-slice_bitcast_fusion.block_ref = f32[2048,1024]{1,0:T(8,128)} fusion(f32[1,2048,4096]{2,1,0:T(8,128)} %param.6, s32[]{:T(128)S(6)} %select_n.62), kind=kLoop, calls=%fused_computation.2 | loop fusion | bytes 16777220 | tf_op jit(solution)/shard_map/dynamic_slice | solution.py:537
  22.4 7.1 %bitcast_multiply_fusion = (f32[1024,2048]{1,0:T(8,128)S(1)}, f32[1024,2048]{1,0:T(8,128)S(1)}) fusion(f32[1,4096,2048]{2,1,0:T(8,128)} %param.7, s32[]{:T(128)S(6)} %select_n.65, f32[8,2048]{1,0:T(8,128)S(1)} %get-tuple-element.230, f32[8,2048]{1,0:T(8,128)S(1)} %get-tuple-element.231, s32[]{:T(128)S(6)} %select_n.63), kind=kLoop, calls=%fused_computation | loop fusion | flops 4194304 | bytes 33685512 | tf_op jit(solution)/shard_map/mul | solution.py:542
  49.2 95.7 %collective-permute-done.16 = f32[512,128]{1,0:T(8,128)S(1)} collective-permute-done((f32[512,128]{1,0:T(8,128)S(1)}, f32[512,128]{1,0:T(8,128)S(1)}, u32[]{:S(2)}, u32[]{:S(2)}) %collective-permute-start.16) | collective-permute-done | bytes 262176 | tf_op jit(solution)/shard_map/ppermute | solution.py:406
  149.5 6.0 %collective-permute-done.17 = f32[512,128]{1,0:T(8,128)S(1)} collective-permute-done((f32[512,128]{1,0:T(8,128)S(1)}, f32[512,128]{1,0:T(8,128)S(1)}, u32[]{:S(2)}, u32[]{:S(2)}) %collective-permute-start.17) | collective-permute-done | bytes 262176 | tf_op jit(solution)/shard_map/ppermute | solution.py:406
  160.4 3.0 collective-permute-start.20
  165.6 6.8 %collective-permute-done.21.refs_1_ = f32[1024,128]{1,0:T(8,128)S(1)} collective-permute-done((f32[1024,128]{1,0:T(8,128)S(1)}, f32[1024,128]{1,0:T(8,128)S(1)}, u32[]{:S(2)}, u32[]{:S(2)}) %collective-permute-start.21) | collective-permute-done | bytes 524320 | tf_op jit(solution)/shard_map/ppermute | solution.py:401
  175.6 3.0 collective-permute-start.23
  178.6 9.5 %shard_map.78.refs_2_ = f32[2048,128]{1,0:T(8,128)S(1)} custom-call(s32[11]{0:T(128)S(1)} %pad_add_fusion.meta, f32[2048,4096]{1,0:T(8,128)} %bitcast.42, f32[1024,128]{1,0:T(8,128)S(1)} %slice_subtract_fusion.refs_0_, f32[1024,128]{1,0:T(8,128)S(1)} %collective-permute-done.21.refs_1_), custom_call_target="tpu_custom_call" | custom-call | flops 1 | bytes 1 | tf_op jit(solution)/shard_map/pallas_call | solution.py:117
  192.6 4.3 %collective-permute-done.28 = f32[512,128]{1,0:T(8,128)S(1)} collective-permute-done((f32[512,128]{1,0:T(8,128)S(1)}, f32[512,128]{1,0:T(8,128)S(1)}, u32[]{:S(2)}, u32[]{:S(2)}) %collective-permute-start.28) | collective-permute-done | bytes 262176 | tf_op jit(solution)/shard_map/ppermute | solution.py:406
  200.9 7.0 %shard_map.79.total_ref = f32[2048,128]{1,0:T(8,128)S(1)} custom-call(s32[11]{0:T(128)S(1)} %pad_add_fusion.meta, f32[2048,4096]{1,0:T(8,128)} %bitcast.43, f32[1024,128]{1,0:T(8,128)S(1)} %collective-permute-done.20.refs_0_, f32[1024,128]{1,0:T(8,128)S(1)} %collective-permute-done.22.refs_1_, f32[2048,128]{1,0:T(8,128)S(1)} %shard_map.78.refs_2_), custom_call_target="tpu_custom_call" | custom-call | flops 1 | bytes 1 | tf_op jit(solution)/shard_map/pallas_call | solution.py:117
  208.1 3.8 %shard_map.80.mine_ref = f32[2048,128]{1,0:T(8,128)S(1)} custom-call(s32[11]{0:T(128)S(1)} %pad_add_fusion.meta, f32[2048,1024]{1,0:T(8,128)S(1)} %bitcast.34, f32[1024,128]{1,0:T(8,128)S(1)} %collective-permute-done.23.inner_ref, f32[1024,128]{1,0:T(8,128)S(1)} %collective-permute-done.32.end_ref, f32[2048,128]{1,0:T(8,128)S(1)} %shard_map.79.total_ref), custom_call_target="tpu_custom_call" | custom-call | flops 1 | bytes 1 | tf_op jit(solution)/shard_map/pallas_call | solution.py:179
  213.9 3.0 collective-permute-start.34
  216.9 4.7 %shard_map.81 = (f32[2048,128]{1,0:T(8,128)S(1)}, bf16[2048,256]{1,0:T(8,128)(2,1)S(1)}, f32[1024,128]{1,0:T(8,128)S(1)}) custom-call(s32[11]{0:T(128)S(1)} %pad_add_fusion.meta, f32[1024,2048]{1,0:T(8,128)S(1)} %get-tuple-element.219.block_ref, f32[2048,128]{1,0:T(8,128)S(1)} %shard_map.80.mine_ref, f32[2048,128]{1,0:T(8,128)S(1)} %collective-permute-done.33.other_ref), custom_call_target="tpu_custom_call" | custom-call | flops 1 | bytes 1 | tf_op jit(solution)/shard_map/pallas_call | solution.py:253
  221.7 6.6 %collective-permute-done.35.refs_1_ = f32[1024,128]{1,0:T(8,128)S(1)} collective-permute-done((f32[1024,128]{1,0:T(8,128)S(1)}, f32[1024,128]{1,0:T(8,128)S(1)}, u32[]{:S(2)}, u32[]{:S(2)}) %collective-permute-start.35) | collective-permute-done | bytes 524320 | tf_op jit(solution)/shard_map/ppermute | solution.py:401
  235.1 4.2 %shard_map.83 = f32[1024,128]{1,0:T(8,128)S(1)} custom-call(s32[11]{0:T(128)S(1)} %pad_add_fusion.meta, f32[1024,2048]{1,0:T(8,128)S(1)} %get-tuple-element.218.block_ref, bf16[2048,256]{1,0:T(8,128)(2,1)S(1)} %get-tuple-element.179.words_ref), custom_call_target="tpu_custom_call" | custom-call | flops 1 | bytes 1 | tf_op jit(solution)/shard_map/pallas_call | solution.py:306
  239.3 9.9 %shard_map.82 = (f32[1024,128]{1,0:T(8,128)S(1)}, f32[1024,128]{1,0:T(8,128)S(1)}) custom-call(s32[11]{0:T(128)S(1)} %pad_add_fusion.meta, f32[4096,2048]{1,0:T(8,128)} %bitcast.47, f32[32,2048]{1,0:T(8,128)S(1)} %bitcast.38, bf16[2048,256]{1,0:T(8,128)(2,1)S(1)} %get-tuple-element.179.words_ref), custom_call_target="tpu_custom_call" | custom-call | flops 1 | bytes 1 | tf_op jit(solution)/shard_map/pallas_call | solution.py:380
  254.2 12.2 %shard_map.84.total_ref = f32[2048,128]{1,0:T(8,128)S(1)} custom-call(s32[11]{0:T(128)S(1)} %pad_add_fusion.meta, f32[2048,4096]{1,0:T(8,128)} %bitcast.44, f32[1024,128]{1,0:T(8,128)S(1)} %maximum_subtract_fusion.refs_0_, f32[1024,128]{1,0:T(8,128)S(1)} %collective-permute-done.35.refs_1_, f32[1024,128]{1,0:T(8,128)S(1)} %collective-permute-done.34.refs_2_, ...), custom_call_target="tpu_custom_call" | custom-call | flops 1 | bytes 1 | tf_op jit(solution)/shard_map/pallas_call | solution.py:117
  266.4 3.8 %shard_map.85.mine_ref = f32[2048,128]{1,0:T(8,128)S(1)} custom-call(s32[11]{0:T(128)S(1)} %pad_add_fusion.meta, f32[2048,1024]{1,0:T(8,128)S(1)} %bitcast.34, f32[1024,128]{1,0:T(8,128)S(1)} %collective-permute-done.36.inner_ref, f32[1024,128]{1,0:T(8,128)S(1)} %collective-permute-done.39.end_ref, f32[2048,128]{1,0:T(8,128)S(1)} %shard_map.84.total_ref), custom_call_target="tpu_custom_call" | custom-call | flops 1 | bytes 1 | tf_op jit(solution)/shard_map/pallas_call | solution.py:179
  275.3 4.7 %shard_map.86 = (f32[2048,128]{1,0:T(8,128)S(1)}, bf16[2048,256]{1,0:T(8,128)(2,1)S(1)}, f32[1024,128]{1,0:T(8,128)S(1)}) custom-call(s32[11]{0:T(128)S(1)} %pad_add_fusion.meta, f32[1024,2048]{1,0:T(8,128)S(1)} %get-tuple-element.219.block_ref, f32[2048,128]{1,0:T(8,128)S(1)} %shard_map.85.mine_ref, f32[2048,128]{1,0:T(8,128)S(1)} %collective-permute-done.40.other_ref), custom_call_target="tpu_custom_call" | custom-call | flops 1 | bytes 1 | tf_op jit(solution)/shard_map/pallas_call | solution.py:253
  280.0 6.6 %collective-permute-done.41 = f32[1024,128]{1,0:T(8,128)S(1)} collective-permute-done((f32[1024,128]{1,0:T(8,128)S(1)}, f32[1024,128]{1,0:T(8,128)S(1)}, u32[]{:S(2)}, u32[]{:S(2)}) %collective-permute-start.41) | collective-permute-done | bytes 524320 | tf_op jit(solution)/shard_map/ppermute | solution.py:401
  289.9 4.2 %shard_map.87 = f32[1024,128]{1,0:T(8,128)S(1)} custom-call(s32[11]{0:T(128)S(1)} %pad_add_fusion.meta, f32[1024,2048]{1,0:T(8,128)S(1)} %get-tuple-element.218.block_ref, bf16[2048,256]{1,0:T(8,128)(2,1)S(1)} %get-tuple-element.206.words_ref), custom_call_target="tpu_custom_call" | custom-call | flops 1 | bytes 1 | tf_op jit(solution)/shard_map/pallas_call | solution.py:306
  294.3 9.7 %collective-permute-done.43 = f32[1024,128]{1,0:T(8,128)S(1)} collective-permute-done((f32[1024,128]{1,0:T(8,128)S(1)}, f32[1024,128]{1,0:T(8,128)S(1)}, u32[]{:S(2)}, u32[]{:S(2)}) %collective-permute-start.43) | collective-permute-done | bytes 524320 | tf_op jit(solution)/shard_map/ppermute | solution.py:401
  308.4 9.7 %shard_map.88 = (f32[1024,128]{1,0:T(8,128)S(1)}, f32[1024,128]{1,0:T(8,128)S(1)}) custom-call(s32[11]{0:T(128)S(1)} %pad_add_fusion.meta, f32[4096,2048]{1,0:T(8,128)} %bitcast.48, f32[32,2048]{1,0:T(8,128)S(1)} %bitcast.39, bf16[2048,256]{1,0:T(8,128)(2,1)S(1)} %get-tuple-element.206.words_ref), custom_call_target="tpu_custom_call" | custom-call | flops 1 | bytes 1 | tf_op jit(solution)/shard_map/pallas_call | solution.py:380
  327.8 6.8 %collective-permute-done.47 = f32[1024,128]{1,0:T(8,128)S(1)} collective-permute-done((f32[1024,128]{1,0:T(8,128)S(1)}, f32[1024,128]{1,0:T(8,128)S(1)}, u32[]{:S(2)}, u32[]{:S(2)}) %collective-permute-start.47) | collective-permute-done | bytes 524320 | tf_op jit(solution)/shard_map/ppermute | solution.py:401
  (148 shorter events, 93.1 us)
Async XLA Ops:
  1.9 14.3 %collective-permute-start.1 = (f32[1024,128]{1,0:T(8,128)S(1)}, f32[1024,128]{1,0:T(8,128)}, u32[]{:S(2)}, u32[]{:S(2)}) collective-permute-start(f32[1024,128]{1,0:T(8,128)S(1)} %get-tuple-element.115.refs_0_), channel_id=1, source_target_pairs={{0,1},{1,0},{2,3},{3,2},{8,9},{9,8},{10,11},{11,10},{16,17},{17,16... | collective-permute-start | bytes 1572872 | tf_op jit(solution)/shard_map/ppermute | solution.py:401
  16.2 13.3 %collective-permute-start.3 = (f32[1024,128]{1,0:T(8,128)}, f32[1024,128]{1,0:T(8,128)}, u32[]{:S(2)}, u32[]{:S(2)}) collective-permute-start(f32[1024,128]{1,0:T(8,128)} %collective-permute-done.1.refs_1_), channel_id=1, source_target_pairs={{1,2},{2,1},{9,10},{10,9},{17,18},{18,17},{5,6},{6,5},{13,14},{14,... | collective-permute-start | bytes 1572872 | tf_op jit(solution)/shard_map/ppermute | solution.py:401
  45.8 99.2 %collective-permute-start.16 = (f32[512,128]{1,0:T(8,128)S(1)}, f32[512,128]{1,0:T(8,128)S(1)}, u32[]{:S(2)}, u32[]{:S(2)}) collective-permute-start(f32[512,128]{1,0:T(8,128)S(1)} %get-tuple-element.228), channel_id=1, source_target_pairs={{0,8},{1,9},{2,10},{3,11},{16,24},{17,25},{18,26},{19,27},{4,12},{... | collective-permute-start | bytes 786440 | tf_op jit(solution)/shard_map/ppermute | solution.py:406
  47.2 99.0 %collective-permute-start.18 = (f32[512,128]{1,0:T(8,128)S(1)}, f32[512,128]{1,0:T(8,128)S(1)}, u32[]{:S(2)}, u32[]{:S(2)}) collective-permute-start(f32[512,128]{1,0:T(8,128)S(1)} %get-tuple-element.229), channel_id=1, source_target_pairs={{0,16},{1,17},{2,18},{3,19},{8,24},{9,25},{10,26},{11,27},{4,20},{... | collective-permute-start | bytes 786440 | tf_op jit(solution)/shard_map/ppermute | solution.py:406
  48.5 108.4 %collective-permute-start.15 = (f32[1024,128]{1,0:T(8,128)S(1)}, f32[1024,128]{1,0:T(8,128)S(1)}, u32[]{:S(2)}, u32[]{:S(2)}) collective-permute-start(f32[1024,128]{1,0:T(8,128)S(1)} %get-tuple-element.161), channel_id=1, source_target_pairs={{0,1},{3,2},{8,9},{11,10},{16,17},{19,18},{4,5},{7,6},{12,13},{15,... | collective-permute-start | bytes 1572872 | tf_op jit(solution)/shard_map/ppermute | solution.py:401
  158.5 13.9 %collective-permute-start.21 = (f32[1024,128]{1,0:T(8,128)S(1)}, f32[1024,128]{1,0:T(8,128)S(1)}, u32[]{:S(2)}, u32[]{:S(2)}) collective-permute-start(f32[1024,128]{1,0:T(8,128)S(1)} %slice_subtract_fusion.refs_0_), channel_id=1, source_target_pairs={{24,25},{25,24},{26,27},{27,26},{28,29},{29,28},{30,31},{31,30}} | collective-permute-start | bytes 1572872 | tf_op jit(solution)/shard_map/ppermute | solution.py:401
  160.4 13.9 %collective-permute-start.20 = (f32[1024,128]{1,0:T(8,128)S(1)}, f32[1024,128]{1,0:T(8,128)S(1)}, u32[]{:S(2)}, u32[]{:S(2)}) collective-permute-start(f32[1024,128]{1,0:T(8,128)S(1)} %slice_subtract_fusion.refs_0_), channel_id=1, source_target_pairs={{25,26},{26,25},{29,30},{30,29}} | collective-permute-start | bytes 1572872 | tf_op jit(solution)/shard_map/ppermute | solution.py:401
  164.1 24.0 %collective-permute-start.27 = (f32[1024,128]{1,0:T(8,128)S(1)}, f32[1024,128]{1,0:T(8,128)S(1)}, u32[]{:S(2)}, u32[]{:S(2)}) collective-permute-start(f32[1024,128]{1,0:T(8,128)S(1)} %add.120), channel_id=1, source_target_pairs={{1,2},{2,1},{9,10},{10,9},{17,18},{18,17},{5,6},{6,5},{13,14},{14,... | collective-permute-start | bytes 1572872 | tf_op jit(solution)/shard_map/ppermute | solution.py:401
  164.9 23.3 %collective-permute-start.26 = (f32[1024,128]{1,0:T(8,128)S(1)}, f32[1024,128]{1,0:T(8,128)S(1)}, u32[]{:S(2)}, u32[]{:S(2)}) collective-permute-start(f32[1024,128]{1,0:T(8,128)S(1)} %add.118), channel_id=1, source_target_pairs={{0,1},{1,0},{2,3},{3,2},{8,9},{9,8},{10,11},{11,10},{16,17},{17,16... | collective-permute-start | bytes 1572872 | tf_op jit(solution)/shard_map/ppermute | solution.py:401
  174.3 13.9 %collective-permute-start.22 = (f32[1024,128]{1,0:T(8,128)S(1)}, f32[1024,128]{1,0:T(8,128)S(1)}, u32[]{:S(2)}, u32[]{:S(2)}) collective-permute-start(f32[1024,128]{1,0:T(8,128)S(1)} %collective-permute-done.20.refs_0_), channel_id=1, source_target_pairs={{25,24},{26,27},{29,28},{30,31}} | collective-permute-start | bytes 1572872 | tf_op jit(solution)/shard_map/ppermute | solution.py:401
  191.3 16.8 %collective-permute-start.32 = (f32[1024,128]{1,0:T(8,128)S(1)}, f32[1024,128]{1,0:T(8,128)S(1)}, u32[]{:S(2)}, u32[]{:S(2)}) collective-permute-start(f32[1024,128]{1,0:T(8,128)S(1)} %collective-permute-done.23.inner_ref), channel_id=1, source_target_pairs={{25,24},{26,27},{29,28},{30,31}} | collective-permute-start | bytes 1572872 | tf_op jit(solution)/shard_map/ppermute | solution.py:401
  212.0 16.2 %collective-permute-start.35 = (f32[1024,128]{1,0:T(8,128)S(1)}, f32[1024,128]{1,0:T(8,128)S(1)}, u32[]{:S(2)}, u32[]{:S(2)}) collective-permute-start(f32[1024,128]{1,0:T(8,128)S(1)} %maximum_subtract_fusion.refs_0_), channel_id=1, source_target_pairs={{24,25},{25,24},{26,27},{27,26},{28,29},{29,28},{30,31},{31,30}} | collective-permute-start | bytes 1572872 | tf_op jit(solution)/shard_map/ppermute | solution.py:401
  213.9 16.2 %collective-permute-start.34 = (f32[1024,128]{1,0:T(8,128)S(1)}, f32[1024,128]{1,0:T(8,128)S(1)}, u32[]{:S(2)}, u32[]{:S(2)}) collective-permute-start(f32[1024,128]{1,0:T(8,128)S(1)} %maximum_subtract_fusion.refs_0_), channel_id=1, source_target_pairs={{25,26},{26,25},{29,30},{30,29}} | collective-permute-start | bytes 1572872 | tf_op jit(solution)/shard_map/ppermute | solution.py:401
  230.2 19.0 %collective-permute-start.37 = (f32[1024,128]{1,0:T(8,128)S(1)}, f32[1024,128]{1,0:T(8,128)S(1)}, u32[]{:S(2)}, u32[]{:S(2)}) collective-permute-start(f32[1024,128]{1,0:T(8,128)S(1)} %broadcast_select_fusion.4), channel_id=1, source_target_pairs={{24,25},{25,24},{26,27},{27,26},{28,29},{29,28},{30,31},{31,30}} | collective-permute-start | bytes 1572872 | tf_op jit(solution)/shard_map/ppermute | solution.py:401
  232.1 17.1 %collective-permute-start.36 = (f32[1024,128]{1,0:T(8,128)S(1)}, f32[1024,128]{1,0:T(8,128)S(1)}, u32[]{:S(2)}, u32[]{:S(2)}) collective-permute-start(f32[1024,128]{1,0:T(8,128)S(1)} %collective-permute-done.35.refs_1_), channel_id=1, source_target_pairs={{25,26},{26,25},{29,30},{30,29}} | collective-permute-start | bytes 1572872 | tf_op jit(solution)/shard_map/ppermute | solution.py:401
  249.3 17.1 %collective-permute-start.39 = (f32[1024,128]{1,0:T(8,128)S(1)}, f32[1024,128]{1,0:T(8,128)S(1)}, u32[]{:S(2)}, u32[]{:S(2)}) collective-permute-start(f32[1024,128]{1,0:T(8,128)S(1)} %broadcast_select_fusion.3), channel_id=1, source_target_pairs={{24,25},{25,24},{26,27},{27,26},{28,29},{29,28},{30,31},{31,30}} | collective-permute-start | bytes 1572872 | tf_op jit(solution)/shard_map/ppermute | solution.py:401
  251.3 15.1 %collective-permute-start.38 = (f32[1024,128]{1,0:T(8,128)S(1)}, f32[1024,128]{1,0:T(8,128)S(1)}, u32[]{:S(2)}, u32[]{:S(2)}) collective-permute-start(f32[1024,128]{1,0:T(8,128)S(1)} %add.126), channel_id=1, source_target_pairs={{25,26},{26,25},{29,30},{30,29}} | collective-permute-start | bytes 1572872 | tf_op jit(solution)/shard_map/ppermute | solution.py:401
  270.4 16.2 %collective-permute-start.41 = (f32[1024,128]{1,0:T(8,128)S(1)}, f32[1024,128]{1,0:T(8,128)S(1)}, u32[]{:S(2)}, u32[]{:S(2)}) collective-permute-start(f32[1024,128]{1,0:T(8,128)S(1)} %add.127), channel_id=1, source_target_pairs={{24,25},{25,24},{26,27},{27,26},{28,29},{29,28},{30,31},{31,30}} | collective-permute-start | bytes 1572872 | tf_op jit(solution)/shard_map/ppermute | solution.py:401
  272.4 16.2 %collective-permute-start.42 = (f32[1024,128]{1,0:T(8,128)S(1)}, f32[1024,128]{1,0:T(8,128)S(1)}, u32[]{:S(2)}, u32[]{:S(2)}) collective-permute-start(f32[1024,128]{1,0:T(8,128)S(1)} %add.128), channel_id=1, source_target_pairs={{25,26},{26,25},{29,30},{30,29}} | collective-permute-start | bytes 1572872 | tf_op jit(solution)/shard_map/ppermute | solution.py:401
  288.6 15.4 %collective-permute-start.43 = (f32[1024,128]{1,0:T(8,128)S(1)}, f32[1024,128]{1,0:T(8,128)S(1)}, u32[]{:S(2)}, u32[]{:S(2)}) collective-permute-start(f32[1024,128]{1,0:T(8,128)S(1)} %get-tuple-element.209), channel_id=1, source_target_pairs={{24,25},{27,26},{28,29},{31,30}} | collective-permute-start | bytes 1572872 | tf_op jit(solution)/shard_map/ppermute | solution.py:401
  304.1 14.5 %collective-permute-start.44 = (f32[1024,128]{1,0:T(8,128)S(1)}, f32[1024,128]{1,0:T(8,128)S(1)}, u32[]{:S(2)}, u32[]{:S(2)}) collective-permute-start(f32[1024,128]{1,0:T(8,128)S(1)} %add.131), channel_id=1, source_target_pairs={{25,26},{26,25},{29,30},{30,29}} | collective-permute-start | bytes 1572872 | tf_op jit(solution)/shard_map/ppermute | solution.py:401
  307.0 14.3 %collective-permute-start.45 = (f32[1024,128]{1,0:T(8,128)S(1)}, f32[1024,128]{1,0:T(8,128)S(1)}, u32[]{:S(2)}, u32[]{:S(2)}) collective-permute-start(f32[1024,128]{1,0:T(8,128)S(1)} %shard_map.87), channel_id=1, source_target_pairs={{24,25},{27,26},{28,29},{31,30}} | collective-permute-start | bytes 1572872 | tf_op jit(solution)/shard_map/ppermute | solution.py:401
  321.3 13.3 %collective-permute-start.47 = (f32[1024,128]{1,0:T(8,128)S(1)}, f32[1024,128]{1,0:T(8,128)S(1)}, u32[]{:S(2)}, u32[]{:S(2)}) collective-permute-start(f32[1024,128]{1,0:T(8,128)S(1)} %add.134), channel_id=1, source_target_pairs={{25,26},{26,25},{29,30},{30,29}} | collective-permute-start | bytes 1572872 | tf_op jit(solution)/shard_map/ppermute | solution.py:401
  324.3 13.1 %collective-permute-start.46 = (f32[1024,128]{1,0:T(8,128)S(1)}, f32[1024,128]{1,0:T(8,128)S(1)}, u32[]{:S(2)}, u32[]{:S(2)}) collective-permute-start(f32[1024,128]{1,0:T(8,128)S(1)} %add.132), channel_id=1, source_target_pairs={{24,25},{25,24},{26,27},{27,26},{28,29},{29,28},{30,31},{31,30}} | collective-permute-start | bytes 1572872 | tf_op jit(solution)/shard_map/ppermute | solution.py:401
  (27 other events, 264.5 us)

commit v3 on v2

v3 whole, which is shorter than its diff:
```python
import functools

import jax
import jax.numpy as jnp
from jax import lax
from jax.experimental import pallas as pl
from jax.experimental.pallas import tpu as pltpu
from jax.sharding import PartitionSpec as P

F32 = jnp.float32
BF16 = jnp.bfloat16
AXES = ("sec", "col")
VMEM_LIMIT = 20 * 1024 * 1024
SWAPS = 3
AT_END, ORDER, SHARD = 2, 3, 7
COST = pl.CostEstimate(flops=1, bytes_accessed=1, transcendentals=0)


def split_words(value):
    high = value.astype(BF16)
    low = (value - high.astype(F32)).astype(BF16)
    return high, low


def three_term(tile, words, width):
    high, low = split_words(tile)
    both = jnp.dot(high, words, preferred_element_type=F32) + jnp.dot(low, words, preferred_element_type=F32)
    return both[:, :width] + both[:, width:]


IN_PLACE = pl.BlockSpec(memory_space=pltpu.VMEM)
ANYWHERE = pl.BlockSpec(memory_space=pl.ANY)
SCALARS = pl.BlockSpec(memory_space=pltpu.SMEM)
PARAMS = pltpu.CompilerParams(vmem_limit_bytes=VMEM_LIMIT)


def tiled(t, tile):
    return pl.ds(pl.multiple_of(t * tile, tile), tile)


def fill(words, at, values):
    rows, width = values.shape
    high, low = split_words(values)
    words[at : at + rows, :width] = high
    words[at : at + rows, width:] = low


def fill_for_chip(meta, words, at, refs):
    if len(refs) == 1:
        fill(words, at, refs[0][...])
    else:
        for end, ref in enumerate(refs):
            pl.when(meta[AT_END] == end)(lambda ref=ref: fill(words, at, ref[...]))


def pieces_body(role, pieces_at, counts, started, meta, factor_ref, *refs):
    n_ops = sum(counts)
    ops, refs = refs[:n_ops], refs[n_ops:]
    if started:
        total_ref, refs = refs[0], refs[1:]
    out_ref, panel, words, panel_sem = refs
    pieces = len(counts)
    slots, tile, joined = panel.shape
    tiles = factor_ref.shape[0] // tile
    depth, width = joined // pieces, out_ref.shape[1]

    @pl.when(meta[role] == 1)
    def _():
        def tile_copy(p, t):
            column = pl.multiple_of(meta[ORDER + pieces_at[p]] * depth, depth)
            return pltpu.make_async_copy(
                factor_ref.at[tiled(t, tile), pl.ds(column, depth)],
                panel.at[t % slots, :, pl.ds(p * depth, depth)],
                panel_sem.at[p, t % slots],
            )

        for t in range(slots):
            for p in range(pieces):
                tile_copy(p, t).start()
        at = 0
        for p, count in enumerate(counts):
            fill_for_chip(meta, words, p * depth, ops[at : at + count])
            at += count

        @pl.loop(0, tiles)
        def _(t):
            for p in range(pieces):
                tile_copy(p, t).wait()
            value = three_term(panel[t % slots], words[...], width)
            rows = tiled(t, tile)
            out_ref[rows, :] = value + total_ref[rows, :] if started else value

            @pl.when(t + slots < tiles)
            def _():
                for p in range(pieces):
                    tile_copy(p, t + slots).start()


def factor_pieces(role, meta, pieces_at, factor, operands, total):
    rows = factor.shape[0]
    depth, width = operands[0][0].shape
    counts = tuple(len(group) for group in operands)
    n_pieces = len(counts)
    tile = min(rows, 256)
    slots = min(rows // tile, 4)
    started = total is not None
    flat = [ref for group in operands for ref in group] + ([total] if started else [])
    return pl.pallas_call(
        functools.partial(pieces_body, role, pieces_at, counts, started),
        out_shape=jax.ShapeDtypeStruct((rows, width), F32),
        in_specs=[SCALARS, ANYWHERE] + [IN_PLACE] * len(flat),
        out_specs=IN_PLACE,
        scratch_shapes=[
            pltpu.VMEM((slots, tile, n_pieces * depth), F32),
            pltpu.VMEM((n_pieces * depth, 2 * width), BF16),
            pltpu.SemaphoreType.DMA((n_pieces, slots)),
        ],
        compiler_params=PARAMS,
        cost_estimate=COST,
    )(meta, factor, *flat)


def last_body(role, meta, block_ref, inner_ref, end_ref, total_ref, out_ref, words):
    rows, width = out_ref.shape
    tile = min(rows, 512)

    @pl.when(meta[role] == 1)
    def _():
        fill_for_chip(meta, words, 0, (inner_ref, end_ref))

        @pl.loop(0, rows // tile)
        def _(t):
            at = tiled(t, tile)
            out_ref[at, :] = three_term(block_ref[at, :], words[...], width) + total_ref[at, :]


def last_piece(role, meta, block, inner, end, total):
    depth, width = inner.shape
    return pl.pallas_call(
        functools.partial(last_body, role),
        out_shape=jax.ShapeDtypeStruct(total.shape, F32),
        in_specs=[SCALARS] + [IN_PLACE] * 4,
        out_specs=IN_PLACE,
        scratch_shapes=[pltpu.VMEM((depth, 2 * width), BF16)],
        compiler_params=PARAMS,
        cost_estimate=COST,
    )(meta, block, inner, end, total)


def masked_terms(panel, mask_ref, words, base, block_rows, width):
    parts = []
    for j in range(panel.shape[0] // block_rows):
        block = panel[j * block_rows : (j + 1) * block_rows, :] * mask_ref[pl.ds(base + j, 1), :]
        parts.append(three_term(block, words, width))
    return parts


def first_body(role, meta, block_ref, mine_ref, *refs):
    others, (solved_ref, words_ref, out_ref) = refs[:-3], refs[-3:]
    rows, width = out_ref.shape
    tile = min(rows, 512)

    @pl.when(meta[role] == 1)
    def _():
        at = 0
        for other in others:
            part = mine_ref[at : at + other.shape[0], :] + other[...]
            solved_ref[at : at + other.shape[0], :] = part
            fill(words_ref, at, part)
            at += other.shape[0]

        @pl.loop(0, rows // tile)
        def _(t):
            at = tiled(t, tile)
            out_ref[at, :] = three_term(block_ref[at, :], words_ref[...], width)


def panel_first(role, meta, block, mine, others):
    depth, width = mine.shape
    return pl.pallas_call(
        functools.partial(first_body, role),
        out_shape=(
            jax.ShapeDtypeStruct((depth, width), F32),
            jax.ShapeDtypeStruct((depth, 2 * width), BF16),
            jax.ShapeDtypeStruct((block.shape[0], width), F32),
        ),
        in_specs=[SCALARS] + [IN_PLACE] * (2 + len(others)),
        out_specs=(IN_PLACE,) * 3,
        compiler_params=PARAMS,
        cost_estimate=COST,
    )(meta, block, mine, *others)


def rest_body(role, ahead, blocks, meta, panel_ref, mask_ref, words_ref, *refs):
    block_refs, outs, (panel, panel_sem) = refs[:blocks], refs[blocks:-2], refs[-2:]
    n_out = len(outs)
    slots, tile, depth = panel.shape
    rows, width = outs[0].shape
    tiles = rows // tile
    block_rows = panel_ref.shape[0] // mask_ref.shape[0]
    per = tile // block_rows

    @pl.when(meta[role] == 1)
    def _():
        def tile_copy(k, t):
            at = tiled(meta[SHARD + ahead + k] * tiles + t, tile)
            slot = ((k - blocks) * tiles + t) % slots
            return pltpu.make_async_copy(panel_ref.at[at], panel.at[slot], panel_sem.at[slot])

        if n_out > blocks:
            for n in range(slots):
                tile_copy(blocks + n // tiles, n % tiles).start()
        for k in range(blocks):

            @pl.loop(0, tiles)
            def _(t):
                at = tiled(t, tile)
                outs[k][at, :] = three_term(block_refs[k][at, :], words_ref[...], width)

        for k in range(blocks, n_out):

            @pl.loop(0, tiles)
            def _(t):
                tile_copy(k, t).wait()
                slot = ((k - blocks) * tiles + t) % slots
                base = (meta[SHARD + ahead + k] * tiles + t) * per
                for j, part in enumerate(masked_terms(panel[slot], mask_ref, words_ref[...], base, block_rows, width)):
                    at = pl.multiple_of(t * tile + j * block_rows, block_rows)
                    outs[k][pl.ds(at, block_rows), :] = part
                if k + slots // tiles < n_out:
                    tile_copy(k + slots // tiles, t).start()


def panel_rest(role, meta, n, ahead, n_out, panel, mask, words, blocks):
    depth, wide = words.shape
    rows = panel.shape[0] // n
    tile = min(rows, 256)
    slots = rows // tile
    return pl.pallas_call(
        functools.partial(rest_body, role, ahead, len(blocks)),
        out_shape=tuple(jax.ShapeDtypeStruct((rows, wide // 2), F32) for _ in range(n_out)),
        in_specs=[SCALARS, ANYWHERE] + [IN_PLACE] * (2 + len(blocks)),
        out_specs=(IN_PLACE,) * n_out,
        scratch_shapes=[pltpu.VMEM((slots, tile, depth), F32), pltpu.SemaphoreType.DMA((slots,))],
        compiler_params=PARAMS,
        cost_estimate=COST,
    )(meta, panel, mask, words, *blocks)


def send(value, secs, pairs):
    n = lax.axis_size("col")
    return lax.ppermute(value, AXES, [(s * n + a, s * n + b) for s in secs for a, b in pairs])


def hop(value, pairs):
    n = lax.axis_size("col")
    return lax.ppermute(value, AXES, [(a * n + c, b * n + c) for a, b in pairs for c in range(n)])


EDGES = ((0, 1), (1, 0), (2, 3), (3, 2))
MIDDLE = ((1, 2), (2, 1))
INWARD = ((1, 0), (2, 3))
OUTWARD = ((0, 1), (3, 2))
ARRIVE = ((0, 1, 2, 3), (1, 0, 2, 3), (2, 3, 1, 0), (3, 2, 1, 0))
LEAVE = ((3, 2, 1, 0), (3, 2, 0, 1), (0, 1, 3, 2), (0, 1, 2, 3))


class Order:
    def __init__(self):
        self.noted = ()

    def step(self, *operands):
        tied = lax.optimization_barrier((*operands, *self.noted))
        self.noted = ()
        return tied[: len(operands)]

    def note(self, *results):
        self.noted += results
        return results if len(results) > 1 else results[0]


class Line:
    def __init__(self, role, secs, meta, inner, factor, panel, mask, blocks):
        self.role, self.secs, self.meta, self.inner = role, secs, meta, inner
        self.factor, self.panel, self.mask, self.blocks = factor, panel, mask, blocks

    def send(self, value, pairs):
        return send(value, self.secs, pairs)

    def solve(self, pieces_at, operands, total):
        return factor_pieces(self.role, self.meta, pieces_at, self.factor, operands, total)

    def swap(self, value):
        step = -(-value.shape[0] // (SWAPS * 16)) * 16
        parts = [value[at : at + step] for at in range(0, value.shape[0], step)]
        return [lax.ppermute(part, "row", [(0, 1), (1, 0)]) for part in parts]

    def last(self, inner, end, total):
        return last_piece(self.role, self.meta, self.blocks[0], inner, end, total)

    def first(self, mine, others):
        return panel_first(self.role, self.meta, self.blocks[1], mine, others)

    def rest(self, words, ahead, n_out, blocks):
        return panel_rest(self.role, self.meta, len(LEAVE), ahead, n_out, self.panel, self.mask, words, blocks)

    def both(self, inner, end):
        return jnp.where(self.inner, inner, end)

    def pair(self, own_a, raw_b, to_b, passed):
        order = Order()
        side_a, mid_a = order.note(self.send(own_a, EDGES), self.send(own_a, MIDDLE))
        prepare = len(self.blocks) == 2
        if prepare:
            late, early = self.blocks
            late = late(self.meta)
            mid_a, side_a, self.meta, self.mask, late = order.step(mid_a, side_a, self.meta, self.mask, late)
            self.blocks = order.note(late, early(self.meta, self.mask, 0), early(self.meta, self.mask, 1))
        else:
            mid_a, side_a, own_a = order.step(mid_a, side_a, own_a)
        near_a, across_a = order.note(self.send(mid_a, INWARD), self.send(side_a, MIDDLE))
        tot_a = None if prepare else order.note(self.solve((0, 1), [[own_a], [side_a]], None))
        own_a, side_a, mid_a, near_a, across_a, raw_b = order.step(own_a, side_a, mid_a, near_a, across_a, raw_b)
        far_a = order.note(self.send(across_a, INWARD))
        if prepare:
            tot_a = order.note(self.solve((0, 1, 2), [[own_a], [side_a], [mid_a, near_a]], None))
        else:
            tot_a = order.note(self.solve((2,), [[mid_a, near_a]], tot_a))
        own_b, tot_a, across_a, far_a = order.step(to_b(raw_b), tot_a, across_a, far_a)
        side_b, mid_b = order.note(self.send(own_b, EDGES), self.send(own_b, MIDDLE))
        tot_a = self.last(across_a, far_a, tot_a)
        solved_a, words_a, r0_a = order.note(*self.first(tot_a, self.swap(tot_a)))
        mid_b, side_b, r0_a, words_a = order.step(mid_b, side_b, r0_a, words_a)
        near_b, across_b = order.note(self.send(self.both(mid_b, r0_a), EDGES), self.send(side_b, MIDDLE))
        r1_a, r2_a, rown_a = order.note(*self.rest(words_a, 1, 3, self.blocks[2:]))
        across_b, r0_a, r1_a, near_b, own_b, side_b, mid_b = order.step(
            across_b, r0_a, r1_a, near_b, own_b, side_b, mid_b
        )
        far_b = order.note(self.send(self.both(across_b, r1_a), EDGES))
        got_a = order.note(self.send(r0_a + near_b, MIDDLE))
        tot_b = order.note(self.solve((0, 1, 2), [[own_b], [side_b], [mid_b, near_b]], None))
        r2_a, got_a, r1_a, far_b, tot_b, across_b = order.step(r2_a, got_a, r1_a, far_b, tot_b, across_b)
        rs_a, rm_a = order.note(self.send(r2_a + got_a, EDGES), self.send(r1_a + far_b, MIDDLE))
        tot_b = self.last(across_b, far_b, tot_b)
        solved_b, words_b, r0_b = order.note(*self.first(tot_b, self.swap(tot_b)))
        r0_b, words_b, rown_a, rs_a, rm_a = order.step(r0_b, words_b, rown_a, rs_a, rm_a)
        sent_a = rown_a + rs_a + rm_a
        near = order.note(self.send(r0_b, OUTWARD))
        passed_a = passed(sent_a)
        r1_b = order.note(*self.rest(words_b, 1, 1, self.blocks[2:]))
        r0_b, near, r1_b, passed_a, words_b = order.step(r0_b, near, r1_b, passed_a, words_b)
        far, got = order.note(self.send(r1_b, OUTWARD), self.send(r0_b + near, MIDDLE))
        r2_b, rown_b = order.note(*self.rest(words_b, 2, 2, ()))
        r2_b, got, r1_b, far = order.step(r2_b, got, r1_b, far)
        rs_b, rm_b = self.send(r2_b + got, EDGES), self.send(r1_b + far, MIDDLE)
        sent_b = rown_b + rs_b + rm_b
        return solved_a, sent_a, solved_b, sent_b, passed_a


def to_last(sent):
    half = sent.shape[0] // 2
    upper, lower = sent[:half], sent[half:]
    got_upper = hop(upper, ((0, 1), (2, 3)))
    got_lower = hop(lower, ((0, 2), (1, 3)))
    sum_upper = hop(upper + got_upper, ((1, 3),))
    sum_lower = hop(lower + got_lower, ((2, 3),))
    return jnp.concatenate([got_upper + sum_upper, got_lower + sum_lower], axis=0)


def shards_line(rhs, inv_factor, coupling, pattern):
    top = lax.axis_size("sec") - 1
    factor, panel = inv_factor[0], coupling[0]
    mask = jnp.repeat(pattern[0].astype(F32), panel.shape[1] // pattern.shape[2], axis=1)
    is_parent = lax.axis_index("sec") == top
    col = lax.axis_index("col")
    inner = (col != 0) & (col != lax.axis_size("col") - 1)
    flags = jnp.stack([~is_parent, is_parent, ~inner]).astype(jnp.int32)
    orders = jnp.asarray([a + b for a, b in zip(ARRIVE, LEAVE)], jnp.int32)
    meta = jnp.concatenate([flags, orders[col]])

    height = panel.shape[0] // len(LEAVE)
    per = height * mask.shape[0] // panel.shape[0]

    def late(meta):
        depth = rhs.shape[1]
        return lax.dynamic_slice(factor, (0, meta[ORDER + 3] * depth), (factor.shape[0], depth))

    def early(meta, mask, k):
        rows = lax.dynamic_slice(panel, (meta[SHARD + k] * height, 0), (height, panel.shape[1]))
        cover = lax.dynamic_slice(mask, (meta[SHARD + k] * per, 0), (per, panel.shape[1]))
        rows = rows.reshape(per, height // per, panel.shape[1]) * cover[:, None, :]
        return rows.reshape(height, panel.shape[1])

    kids = Line(0, tuple(range(top)), meta, inner, factor, panel, mask, (late, early))
    half = rhs.shape[2] // 2
    own = [rhs[0][:, :half], rhs[0][:, half:]]
    solved0, sent0, solved1, sent1, passed0 = kids.pair(own[0], own[1], lambda rows: rows, to_last)
    head = Line(1, (top,), kids.meta, inner, factor, panel, kids.mask, kids.blocks)
    psolved0, psent0, psolved1, psent1, _ = head.pair(
        own[0] - passed0, sent1, lambda sent: own[1] - to_last(sent), lambda sent: sent
    )
    pick = lambda p, c: jnp.where(is_parent, p, c)
    solution = jnp.concatenate([pick(psolved0, solved0), pick(psolved1, solved1)], axis=1)
    outgoing = jnp.concatenate([pick(psent0, sent0), pick(psent1, sent1)], axis=1)
    return solution[None], outgoing[None]


def shards_any(rhs, inv_factor, coupling, pattern):
    highest = lax.Precision.HIGHEST
    factor = inv_factor[0]
    coupling_local = coupling[0]
    occupancy = pattern[0].astype(jnp.float32)
    block_rows = coupling_local.shape[0] // occupancy.shape[0]
    block_cols = coupling_local.shape[1] // occupancy.shape[1]
    masked = (
        coupling_local.reshape(occupancy.shape[0], block_rows, occupancy.shape[1], block_cols)
        * occupancy[:, None, :, None]
    ).reshape(coupling_local.shape)
    parent_flag = lax.axis_index("sec") == lax.axis_size("sec") - 1

    def segment(rows):
        operand = lax.all_gather(rows, "col", axis=0, tiled=True)
        solved = lax.psum(jnp.dot(factor, operand, precision=highest, preferred_element_type=F32), "row")
        update = jnp.dot(masked, solved, precision=highest, preferred_element_type=F32)
        return solved, lax.psum_scatter(update, "col", scatter_dimension=0, tiled=True)

    solved_a, shares_a = segment(rhs[0])
    total = lax.psum(jnp.where(parent_flag, 0.0, shares_a), "sec")
    solved_b, shares_b = segment(rhs[0] - total)
    solution = jnp.where(parent_flag, solved_b, solved_a)
    outgoing = jnp.where(parent_flag, shares_b, shares_a)
    return (solution[None], outgoing[None])


def solution(mesh):
    placed = (
        P("sec", ("row", "col"), None),
        P("sec", "col", "row"),
        P("sec", "row", "col"),
        P("sec", "row", "col"),
    )
    line = mesh.shape["col"] == 4 and mesh.shape["row"] == 2 and mesh.shape["sec"] == 4
    return jax.shard_map(
        shards_line if line else shards_any,
        mesh=mesh,
        in_specs=placed,
        out_specs=(P("sec", "col", None), P("sec", ("row", "col"), None)),
        check_vma=False,
    )
```

time: 340 us -> 304 us (0.89)
  waiting for transfers between devices: 161 us -> 136 us
  Pallas kernels: 80.4 us -> 66.4 us
  starting transfers between devices: 66.6 us -> 70.7 us
    ppermute x8, waiting for transfers between devices: 110 us -> 89 us  [hop(): lax.ppermute(value, AXES, [(a * n + c, b * n + c) for a, b in pairs for c...]
    ppermute x36, waiting for transfers between devices: 48.8 us -> 39 us  [send(): lax.ppermute(value, AXES, [(s * n + a, s * n + b) for s in secs for a, b...]
    pallas_call x8 -> x6, Pallas kernels: 30.5 us -> 23.5 us  [panel_rest(): pl.pallas_call(functools.partial(rest_body, role, ahead, len(blocks)), ou...]
    ppermute x4 -> x12, waiting for transfers between devices: 2.24 us -> 7.88 us  [swap(): return [lax.ppermute(part, 'row', [(0, 1), (1, 0)]) for part in parts]]
    pallas_call x5, Pallas kernels: 30.2 us -> 26.1 us  [factor_pieces(): pl.pallas_call(functools.partial(pieces_body, role, pieces_at, counts, st...]
  transfers between devices with their start and end apart: 48 -> 56, of which waited for: 21 -> 24; matrix products, arithmetic and copies ran while one was open for 6% -> 7% of each run, Pallas kernels for 21% -> 22%
where the time goes in v3:
time: 304 us; the launch traced here: 303 us
  waiting for transfers between devices  136 us (45%)
  starting transfers between devices  70.7 us (23%)
  Pallas kernels  66.4 us (22%)
  other arithmetic  12.4 us (4%)
  local copies, waits for them, and re-layouts  12.2 us (4%)
  between operations  4.88 us (2%)
    ppermute x8, waiting for transfers between devices, hop(): lax.ppermute(value, AXES, [(a * n + c, b * n + c) for a, b in pairs for c...  89 us
    ppermute x36, starting transfers between devices, send(): lax.ppermute(value, AXES, [(s * n + a, s * n + b) for s in secs for a, b...  57.3 us
    ppermute x36, waiting for transfers between devices, send(): lax.ppermute(value, AXES, [(s * n + a, s * n + b) for s in secs for a, b...  39 us
    pallas_call x5, Pallas kernels, factor_pieces(): pl.pallas_call(functools.partial(pieces_body, role, pieces_at, counts, st...  26.1 us
    pallas_call x6, Pallas kernels, panel_rest(): pl.pallas_call(functools.partial(rest_body, role, ahead, len(blocks)), ou...  23.5 us
    ppermute x8, starting transfers between devices, hop(): lax.ppermute(value, AXES, [(a * n + c, b * n + c) for a, b in pairs for c...  10.5 us
    pallas_call x4, Pallas kernels, last_piece(): pl.pallas_call(functools.partial(last_body, role), out_shape=jax.ShapeDty...  8.93 us
    dynamic_slice x1, local copies, waits for them, and re-layouts, late(): lax.dynamic_slice(factor, (0, meta[ORDER + 3] * depth), (factor.shape[0],...  8.38 us
  transfers between devices with their start and end apart: 56, of which 24 were waited for; matrix products, arithmetic and copies ran while one was open for 7% of the time, Pallas kernels for 22%

profile of v3, /device:TPU:14, one launch (start us, length us, event | category | flops | bytes accessed | tf_op | source)
XLA Modules:
  0.0 302.5 jit_solution(1683534964775282147)
XLA Ops:
  8.0 8.4 %dynamic-slice_bitcast_fusion.block_ref = f32[2048,1024]{1,0:T(8,128)} fusion(f32[1,2048,4096]{2,1,0:T(8,128)} %param.6, s32[]{:T(128)S(6)} %select_n.62), kind=kLoop, calls=%fused_computation.2 | loop fusion | bytes 16777220 | tf_op jit(solution)/shard_map/dynamic_slice | solution.py:386
  22.5 7.1 %bitcast_multiply_fusion = (f32[1024,2048]{1,0:T(8,128)S(1)}, f32[1024,2048]{1,0:T(8,128)S(1)}) fusion(f32[1,4096,2048]{2,1,0:T(8,128)} %param.7, s32[]{:T(128)S(6)} %select_n.65, f32[8,2048]{1,0:T(8,128)S(1)} %get-tuple-element.242, f32[8,2048]{1,0:T(8,128)S(1)} %get-tuple-element.243, s32[]{:T(128)S(6)} %select_n.63), kind=kLoop, calls=%fused_computation | loop fusion | flops 4194304 | bytes 33685512 | tf_op jit(solution)/shard_map/mul | solution.py:391
  51.4 74.2 %collective-permute-done.20 = f32[512,128]{1,0:T(8,128)S(1)} collective-permute-done((f32[512,128]{1,0:T(8,128)S(1)}, f32[512,128]{1,0:T(8,128)S(1)}, u32[]{:S(2)}, u32[]{:S(2)}) %collective-permute-start.20) | collective-permute-done | bytes 262176 | tf_op jit(solution)/shard_map/ppermute | solution.py:257
  130.3 5.0 %collective-permute-done.21 = f32[512,128]{1,0:T(8,128)S(1)} collective-permute-done((f32[512,128]{1,0:T(8,128)S(1)}, f32[512,128]{1,0:T(8,128)S(1)}, u32[]{:S(2)}, u32[]{:S(2)}) %collective-permute-start.21) | collective-permute-done | bytes 262176 | tf_op jit(solution)/shard_map/ppermute | solution.py:257
  138.3 3.2 %collective-permute-start.25 = (f32[1024,128]{1,0:T(8,128)S(1)}, f32[1024,128]{1,0:T(8,128)S(1)}, u32[]{:S(2)}, u32[]{:S(2)}) collective-permute-start(f32[1024,128]{1,0:T(8,128)S(1)} %slice_subtract_fusion.refs_0_), channel_id=1, source_target_pairs={{24,25},{25,24},{26,27},{27,26},{28,29},{29,28},{30,31},{31,30}} | collective-permute-start | bytes 1572872 | tf_op jit(solution)/shard_map/ppermute | solution.py:252
  146.5 5.8 %collective-permute-done.25.refs_1_ = f32[1024,128]{1,0:T(8,128)S(1)} collective-permute-done((f32[1024,128]{1,0:T(8,128)S(1)}, f32[1024,128]{1,0:T(8,128)S(1)}, u32[]{:S(2)}, u32[]{:S(2)}) %collective-permute-start.25) | collective-permute-done | bytes 524320 | tf_op jit(solution)/shard_map/ppermute | solution.py:252
  152.3 3.4 %collective-permute-done.24.refs_0_ = f32[1024,128]{1,0:T(8,128)S(1)} collective-permute-done((f32[1024,128]{1,0:T(8,128)S(1)}, f32[1024,128]{1,0:T(8,128)S(1)}, u32[]{:S(2)}, u32[]{:S(2)}) %collective-permute-start.24) | collective-permute-done | bytes 524320 | tf_op jit(solution)/shard_map/ppermute | solution.py:252
  159.9 7.9 %shard_map.77.refs_2_ = f32[2048,128]{1,0:T(8,128)S(1)} custom-call(s32[11]{0:T(128)S(1)} %pad_add_fusion.meta, f32[2048,4096]{1,0:T(8,128)} %bitcast.50, f32[1024,128]{1,0:T(8,128)S(1)} %slice_subtract_fusion.refs_0_, f32[1024,128]{1,0:T(8,128)S(1)} %collective-permute-done.25.refs_1_), custom_call_target="tpu_custom_call" | custom-call | flops 1 | bytes 1 | tf_op jit(solution)/shard_map/pallas_call | solution.py:108
  174.2 4.3 %collective-permute-done.32 = f32[512,128]{1,0:T(8,128)S(1)} collective-permute-done((f32[512,128]{1,0:T(8,128)S(1)}, f32[512,128]{1,0:T(8,128)S(1)}, u32[]{:S(2)}, u32[]{:S(2)}) %collective-permute-start.32) | collective-permute-done | bytes 262176 | tf_op jit(solution)/shard_map/ppermute | solution.py:257
  182.5 5.4 %shard_map.78.total_ref = f32[2048,128]{1,0:T(8,128)S(1)} custom-call(s32[11]{0:T(128)S(1)} %pad_add_fusion.meta, f32[2048,4096]{1,0:T(8,128)} %bitcast.51, f32[1024,128]{1,0:T(8,128)S(1)} %collective-permute-done.24.refs_0_, f32[1024,128]{1,0:T(8,128)S(1)} %collective-permute-done.26.refs_1_, f32[2048,128]{1,0:T(8,128)S(1)} %shard_map.77.refs_2_), custom_call_target="tpu_custom_call" | custom-call | flops 1 | bytes 1 | tf_op jit(solution)/shard_map/pallas_call | solution.py:108
  194.4 3.6 %shard_map.79.mine_ref = f32[2048,128]{1,0:T(8,128)S(1)} custom-call(s32[11]{0:T(128)S(1)} %pad_add_fusion.meta, f32[2048,1024]{1,0:T(8,128)S(1)} %bitcast.34, f32[1024,128]{1,0:T(8,128)S(1)} %collective-permute-done.27.inner_ref, f32[1024,128]{1,0:T(8,128)S(1)} %collective-permute-done.36.end_ref, f32[2048,128]{1,0:T(8,128)S(1)} %shard_map.78.total_ref), custom_call_target="tpu_custom_call" | custom-call | flops 1 | bytes 1 | tf_op jit(solution)/shard_map/pallas_call | solution.py:139
  200.7 3.4 %shard_map.80 = (f32[2048,128]{1,0:T(8,128)S(1)}, bf16[2048,256]{1,0:T(8,128)(2,1)S(1)}, f32[1024,128]{1,0:T(8,128)S(1)}) custom-call(s32[11]{0:T(128)S(1)} %pad_add_fusion.meta, f32[1024,2048]{1,0:T(8,128)S(1)} %get-tuple-element.223.block_ref, f32[2048,128]{1,0:T(8,128)S(1)} %shard_map.79.mine_ref, f32[688,128]{1,0:T(8,128)S(1)} %collective-permute-done.37.refs_0_, ...), custom_call_target="tpu_custom_call" | custom-call | flops 1 | bytes 1 | tf_op jit(solution)/shard_map/pallas_call | solution.py:180
  206.2 3.0 collective-permute-start.42
  209.2 9.9 %shard_map.81 = (f32[1024,128]{1,0:T(8,128)S(1)}, f32[1024,128]{1,0:T(8,128)S(1)}, f32[1024,128]{1,0:T(8,128)S(1)}) custom-call(s32[11]{0:T(128)S(1)} %pad_add_fusion.meta, f32[4096,2048]{1,0:T(8,128)} %bitcast.45, f32[32,2048]{1,0:T(8,128)S(1)} %bitcast.39, bf16[2048,256]{1,0:T(8,128)(2,1)S(1)} %get-tuple-element.182.words_ref, ...), custom_call_target="tpu_custom_call" | custom-call | flops 1 | bytes 1 | tf_op jit(solution)/shard_map/pallas_call | solution.py:239
  227.1 10.5 %shard_map.82.total_ref = f32[2048,128]{1,0:T(8,128)S(1)} custom-call(s32[11]{0:T(128)S(1)} %pad_add_fusion.meta, f32[2048,4096]{1,0:T(8,128)} %bitcast.52, f32[1024,128]{1,0:T(8,128)S(1)} %maximum_subtract_fusion.refs_0_, f32[1024,128]{1,0:T(8,128)S(1)} %collective-permute-done.41.refs_1_, f32[1024,128]{1,0:T(8,128)S(1)} %collective-permute-done.40.refs_2_, ...), custom_call_target="tpu_custom_call" | custom-call | flops 1 | bytes 1 | tf_op jit(solution)/shard_map/pallas_call | solution.py:108
  241.2 3.0 collective-permute-start.50
  244.2 3.6 %shard_map.83.mine_ref = f32[2048,128]{1,0:T(8,128)S(1)} custom-call(s32[11]{0:T(128)S(1)} %pad_add_fusion.meta, f32[2048,1024]{1,0:T(8,128)S(1)} %bitcast.34, f32[1024,128]{1,0:T(8,128)S(1)} %collective-permute-done.42.inner_ref, f32[1024,128]{1,0:T(8,128)S(1)} %collective-permute-done.45.end_ref, f32[2048,128]{1,0:T(8,128)S(1)} %shard_map.82.total_ref), custom_call_target="tpu_custom_call" | custom-call | flops 1 | bytes 1 | tf_op jit(solution)/shard_map/pallas_call | solution.py:139
  250.5 3.4 %shard_map.84 = (f32[2048,128]{1,0:T(8,128)S(1)}, bf16[2048,256]{1,0:T(8,128)(2,1)S(1)}, f32[1024,128]{1,0:T(8,128)S(1)}) custom-call(s32[11]{0:T(128)S(1)} %pad_add_fusion.meta, f32[1024,2048]{1,0:T(8,128)S(1)} %get-tuple-element.223.block_ref, f32[2048,128]{1,0:T(8,128)S(1)} %shard_map.83.mine_ref, f32[688,128]{1,0:T(8,128)S(1)} %collective-permute-done.46.refs_0_, ...), custom_call_target="tpu_custom_call" | custom-call | flops 1 | bytes 1 | tf_op jit(solution)/shard_map/pallas_call | solution.py:180
  256.5 3.5 %shard_map.85 = f32[1024,128]{1,0:T(8,128)S(1)} custom-call(s32[11]{0:T(128)S(1)} %pad_add_fusion.meta, f32[4096,2048]{1,0:T(8,128)} %bitcast.46, f32[32,2048]{1,0:T(8,128)S(1)} %bitcast.40, bf16[2048,256]{1,0:T(8,128)(2,1)S(1)} %get-tuple-element.210.words_ref, f32[1024,2048]{1,0:T(8,128)S(1)} %get-tuple-element.222.refs_0_), custom_call_target="tpu_custom_call" | custom-call | flops 1 | bytes 1 | tf_op jit(solution)/shard_map/pallas_call | solution.py:239
  260.2 9.6 %collective-permute-done.51 = f32[1024,128]{1,0:T(8,128)S(1)} collective-permute-done((f32[1024,128]{1,0:T(8,128)S(1)}, f32[1024,128]{1,0:T(8,128)S(1)}, u32[]{:S(2)}, u32[]{:S(2)}) %collective-permute-start.51) | collective-permute-done | bytes 524320 | tf_op jit(solution)/shard_map/ppermute | solution.py:252
  274.1 8.3 %shard_map.86 = (f32[1024,128]{1,0:T(8,128)S(1)}, f32[1024,128]{1,0:T(8,128)S(1)}) custom-call(s32[11]{0:T(128)S(1)} %pad_add_fusion.meta, f32[4096,2048]{1,0:T(8,128)} %bitcast.47, f32[32,2048]{1,0:T(8,128)S(1)} %bitcast.41, bf16[2048,256]{1,0:T(8,128)(2,1)S(1)} %get-tuple-element.210.words_ref), custom_call_target="tpu_custom_call" | custom-call | flops 1 | bytes 1 | tf_op jit(solution)/shard_map/pallas_call | solution.py:239
  286.0 3.2 %collective-permute-start.55 = (f32[1024,128]{1,0:T(8,128)S(1)}, f32[1024,128]{1,0:T(8,128)S(1)}, u32[]{:S(2)}, u32[]{:S(2)}) collective-permute-start(f32[1024,128]{1,0:T(8,128)S(1)} %add.134), channel_id=1, source_target_pairs={{25,26},{26,25},{29,30},{30,29}} | collective-permute-start | bytes 1572872 | tf_op jit(solution)/shard_map/ppermute | solution.py:252
  292.7 5.5 %collective-permute-done.55 = f32[1024,128]{1,0:T(8,128)S(1)} collective-permute-done((f32[1024,128]{1,0:T(8,128)S(1)}, f32[1024,128]{1,0:T(8,128)S(1)}, u32[]{:S(2)}, u32[]{:S(2)}) %collective-permute-start.55) | collective-permute-done | bytes 524320 | tf_op jit(solution)/shard_map/ppermute | solution.py:252
  298.2 3.2 %collective-permute-done.54 = f32[1024,128]{1,0:T(8,128)S(1)} collective-permute-done((f32[1024,128]{1,0:T(8,128)S(1)}, f32[1024,128]{1,0:T(8,128)S(1)}, u32[]{:S(2)}, u32[]{:S(2)}) %collective-permute-start.54) | collective-permute-done | bytes 524320 | tf_op jit(solution)/shard_map/ppermute | solution.py:252
  (170 shorter events, 99.3 us)
Async XLA Ops:
  1.9 14.4 %collective-permute-start.1 = (f32[1024,128]{1,0:T(8,128)S(1)}, f32[1024,128]{1,0:T(8,128)}, u32[]{:S(2)}, u32[]{:S(2)}) collective-permute-start(f32[1024,128]{1,0:T(8,128)S(1)} %get-tuple-element.117.refs_0_), channel_id=1, source_target_pairs={{0,1},{1,0},{2,3},{3,2},{8,9},{9,8},{10,11},{11,10},{16,17},{17,16... | collective-permute-start | bytes 1572872 | tf_op jit(solution)/shard_map/ppermute | solution.py:252
  3.4 13.0 %collective-permute-start = (f32[1024,128]{1,0:T(8,128)S(1)}, f32[1024,128]{1,0:T(8,128)}, u32[]{:S(2)}, u32[]{:S(2)}) collective-permute-start(f32[1024,128]{1,0:T(8,128)S(1)} %get-tuple-element.117.refs_0_), channel_id=1, source_target_pairs={{1,2},{2,1},{9,10},{10,9},{17,18},{18,17},{5,6},{6,5},{13,14},{14,... | collective-permute-start | bytes 1572872 | tf_op jit(solution)/shard_map/ppermute | solution.py:252
  16.4 13.3 %collective-permute-start.3 = (f32[1024,128]{1,0:T(8,128)}, f32[1024,128]{1,0:T(8,128)}, u32[]{:S(2)}, u32[]{:S(2)}) collective-permute-start(f32[1024,128]{1,0:T(8,128)} %collective-permute-done.1.refs_1_), channel_id=1, source_target_pairs={{1,2},{2,1},{9,10},{10,9},{17,18},{18,17},{5,6},{6,5},{13,14},{14,... | collective-permute-start | bytes 1572872 | tf_op jit(solution)/shard_map/ppermute | solution.py:252
  48.1 77.5 %collective-permute-start.20 = (f32[512,128]{1,0:T(8,128)S(1)}, f32[512,128]{1,0:T(8,128)S(1)}, u32[]{:S(2)}, u32[]{:S(2)}) collective-permute-start(f32[512,128]{1,0:T(8,128)S(1)} %get-tuple-element.240), channel_id=1, source_target_pairs={{0,8},{1,9},{2,10},{3,11},{16,24},{17,25},{18,26},{19,27},{4,12},{... | collective-permute-start | bytes 786440 | tf_op jit(solution)/shard_map/ppermute | solution.py:257
  49.4 77.5 %collective-permute-start.22 = (f32[512,128]{1,0:T(8,128)S(1)}, f32[512,128]{1,0:T(8,128)S(1)}, u32[]{:S(2)}, u32[]{:S(2)}) collective-permute-start(f32[512,128]{1,0:T(8,128)S(1)} %get-tuple-element.241), channel_id=1, source_target_pairs={{0,16},{1,17},{2,18},{3,19},{8,24},{9,25},{10,26},{11,27},{4,20},{... | collective-permute-start | bytes 786440 | tf_op jit(solution)/shard_map/ppermute | solution.py:257
  50.7 86.1 %collective-permute-start.19 = (f32[1024,128]{1,0:T(8,128)S(1)}, f32[1024,128]{1,0:T(8,128)S(1)}, u32[]{:S(2)}, u32[]{:S(2)}) collective-permute-start(f32[1024,128]{1,0:T(8,128)S(1)} %get-tuple-element.164), channel_id=1, source_target_pairs={{0,1},{3,2},{8,9},{11,10},{16,17},{19,18},{4,5},{7,6},{12,13},{15,... | collective-permute-start | bytes 1572872 | tf_op jit(solution)/shard_map/ppermute | solution.py:252
  138.3 14.0 %collective-permute-start.25 = (f32[1024,128]{1,0:T(8,128)S(1)}, f32[1024,128]{1,0:T(8,128)S(1)}, u32[]{:S(2)}, u32[]{:S(2)}) collective-permute-start(f32[1024,128]{1,0:T(8,128)S(1)} %slice_subtract_fusion.refs_0_), channel_id=1, source_target_pairs={{24,25},{25,24},{26,27},{27,26},{28,29},{29,28},{30,31},{31,30}} | collective-permute-start | bytes 1572872 | tf_op jit(solution)/shard_map/ppermute | solution.py:252
  141.5 14.2 %collective-permute-start.24 = (f32[1024,128]{1,0:T(8,128)S(1)}, f32[1024,128]{1,0:T(8,128)S(1)}, u32[]{:S(2)}, u32[]{:S(2)}) collective-permute-start(f32[1024,128]{1,0:T(8,128)S(1)} %slice_subtract_fusion.refs_0_), channel_id=1, source_target_pairs={{25,26},{26,25},{29,30},{30,29}} | collective-permute-start | bytes 1572872 | tf_op jit(solution)/shard_map/ppermute | solution.py:252
  145.1 22.8 %collective-permute-start.31 = (f32[1024,128]{1,0:T(8,128)S(1)}, f32[1024,128]{1,0:T(8,128)S(1)}, u32[]{:S(2)}, u32[]{:S(2)}) collective-permute-start(f32[1024,128]{1,0:T(8,128)S(1)} %add.120), channel_id=1, source_target_pairs={{1,2},{2,1},{9,10},{10,9},{17,18},{18,17},{5,6},{6,5},{13,14},{14,... | collective-permute-start | bytes 1572872 | tf_op jit(solution)/shard_map/ppermute | solution.py:252
  145.8 22.0 %collective-permute-start.30 = (f32[1024,128]{1,0:T(8,128)S(1)}, f32[1024,128]{1,0:T(8,128)S(1)}, u32[]{:S(2)}, u32[]{:S(2)}) collective-permute-start(f32[1024,128]{1,0:T(8,128)S(1)} %add.118), channel_id=1, source_target_pairs={{0,1},{1,0},{2,3},{3,2},{8,9},{9,8},{10,11},{11,10},{16,17},{17,16... | collective-permute-start | bytes 1572872 | tf_op jit(solution)/shard_map/ppermute | solution.py:252
  157.0 13.2 %collective-permute-start.27 = (f32[1024,128]{1,0:T(8,128)S(1)}, f32[1024,128]{1,0:T(8,128)S(1)}, u32[]{:S(2)}, u32[]{:S(2)}) collective-permute-start(f32[1024,128]{1,0:T(8,128)S(1)} %collective-permute-done.25.refs_1_), channel_id=1, source_target_pairs={{25,26},{26,25},{29,30},{30,29}} | collective-permute-start | bytes 1572872 | tf_op jit(solution)/shard_map/ppermute | solution.py:252
  172.9 16.7 %collective-permute-start.36 = (f32[1024,128]{1,0:T(8,128)S(1)}, f32[1024,128]{1,0:T(8,128)S(1)}, u32[]{:S(2)}, u32[]{:S(2)}) collective-permute-start(f32[1024,128]{1,0:T(8,128)S(1)} %collective-permute-done.27.inner_ref), channel_id=1, source_target_pairs={{25,24},{26,27},{29,28},{30,31}} | collective-permute-start | bytes 1572872 | tf_op jit(solution)/shard_map/ppermute | solution.py:252
  189.6 14.5 %collective-permute-start.41 = (f32[1024,128]{1,0:T(8,128)S(1)}, f32[1024,128]{1,0:T(8,128)S(1)}, u32[]{:S(2)}, u32[]{:S(2)}) collective-permute-start(f32[1024,128]{1,0:T(8,128)S(1)} %maximum_subtract_fusion.refs_0_), channel_id=1, source_target_pairs={{24,25},{25,24},{26,27},{27,26},{28,29},{29,28},{30,31},{31,30}} | collective-permute-start | bytes 1572872 | tf_op jit(solution)/shard_map/ppermute | solution.py:252
  191.5 12.6 %collective-permute-start.40 = (f32[1024,128]{1,0:T(8,128)S(1)}, f32[1024,128]{1,0:T(8,128)S(1)}, u32[]{:S(2)}, u32[]{:S(2)}) collective-permute-start(f32[1024,128]{1,0:T(8,128)S(1)} %maximum_subtract_fusion.refs_0_), channel_id=1, source_target_pairs={{25,26},{26,25},{29,30},{30,29}} | collective-permute-start | bytes 1572872 | tf_op jit(solution)/shard_map/ppermute | solution.py:252
  204.2 15.9 %collective-permute-start.43 = (f32[1024,128]{1,0:T(8,128)S(1)}, f32[1024,128]{1,0:T(8,128)S(1)}, u32[]{:S(2)}, u32[]{:S(2)}) collective-permute-start(f32[1024,128]{1,0:T(8,128)S(1)} %broadcast_select_fusion.4), channel_id=1, source_target_pairs={{24,25},{25,24},{26,27},{27,26},{28,29},{29,28},{30,31},{31,30}} | collective-permute-start | bytes 1572872 | tf_op jit(solution)/shard_map/ppermute | solution.py:252
  206.2 15.9 %collective-permute-start.42 = (f32[1024,128]{1,0:T(8,128)S(1)}, f32[1024,128]{1,0:T(8,128)S(1)}, u32[]{:S(2)}, u32[]{:S(2)}) collective-permute-start(f32[1024,128]{1,0:T(8,128)S(1)} %collective-permute-done.41.refs_1_), channel_id=1, source_target_pairs={{25,26},{26,25},{29,30},{30,29}} | collective-permute-start | bytes 1572872 | tf_op jit(solution)/shard_map/ppermute | solution.py:252
  222.1 15.5 %collective-permute-start.45 = (f32[1024,128]{1,0:T(8,128)S(1)}, f32[1024,128]{1,0:T(8,128)S(1)}, u32[]{:S(2)}, u32[]{:S(2)}) collective-permute-start(f32[1024,128]{1,0:T(8,128)S(1)} %broadcast_select_fusion.3), channel_id=1, source_target_pairs={{24,25},{25,24},{26,27},{27,26},{28,29},{29,28},{30,31},{31,30}} | collective-permute-start | bytes 1572872 | tf_op jit(solution)/shard_map/ppermute | solution.py:252
  224.1 15.0 %collective-permute-start.44 = (f32[1024,128]{1,0:T(8,128)S(1)}, f32[1024,128]{1,0:T(8,128)S(1)}, u32[]{:S(2)}, u32[]{:S(2)}) collective-permute-start(f32[1024,128]{1,0:T(8,128)S(1)} %add.126), channel_id=1, source_target_pairs={{25,26},{26,25},{29,30},{30,29}} | collective-permute-start | bytes 1572872 | tf_op jit(solution)/shard_map/ppermute | solution.py:252
  239.2 14.8 %collective-permute-start.49 = (f32[1024,128]{1,0:T(8,128)S(1)}, f32[1024,128]{1,0:T(8,128)S(1)}, u32[]{:S(2)}, u32[]{:S(2)}) collective-permute-start(f32[1024,128]{1,0:T(8,128)S(1)} %add.127), channel_id=1, source_target_pairs={{24,25},{25,24},{26,27},{27,26},{28,29},{29,28},{30,31},{31,30}} | collective-permute-start | bytes 1572872 | tf_op jit(solution)/shard_map/ppermute | solution.py:252
  241.2 14.1 %collective-permute-start.50 = (f32[1024,128]{1,0:T(8,128)S(1)}, f32[1024,128]{1,0:T(8,128)S(1)}, u32[]{:S(2)}, u32[]{:S(2)}) collective-permute-start(f32[1024,128]{1,0:T(8,128)S(1)} %add.128), channel_id=1, source_target_pairs={{25,26},{26,25},{29,30},{30,29}} | collective-permute-start | bytes 1572872 | tf_op jit(solution)/shard_map/ppermute | solution.py:252
  255.3 14.6 %collective-permute-start.51 = (f32[1024,128]{1,0:T(8,128)S(1)}, f32[1024,128]{1,0:T(8,128)S(1)}, u32[]{:S(2)}, u32[]{:S(2)}) collective-permute-start(f32[1024,128]{1,0:T(8,128)S(1)} %get-tuple-element.213), channel_id=1, source_target_pairs={{24,25},{27,26},{28,29},{31,30}} | collective-permute-start | bytes 1572872 | tf_op jit(solution)/shard_map/ppermute | solution.py:252
  269.9 13.7 %collective-permute-start.52 = (f32[1024,128]{1,0:T(8,128)S(1)}, f32[1024,128]{1,0:T(8,128)S(1)}, u32[]{:S(2)}, u32[]{:S(2)}) collective-permute-start(f32[1024,128]{1,0:T(8,128)S(1)} %add.131), channel_id=1, source_target_pairs={{25,26},{26,25},{29,30},{30,29}} | collective-permute-start | bytes 1572872 | tf_op jit(solution)/shard_map/ppermute | solution.py:252
  272.7 13.2 %collective-permute-start.53 = (f32[1024,128]{1,0:T(8,128)S(1)}, f32[1024,128]{1,0:T(8,128)S(1)}, u32[]{:S(2)}, u32[]{:S(2)}) collective-permute-start(f32[1024,128]{1,0:T(8,128)S(1)} %shard_map.85), channel_id=1, source_target_pairs={{24,25},{27,26},{28,29},{31,30}} | collective-permute-start | bytes 1572872 | tf_op jit(solution)/shard_map/ppermute | solution.py:252
  286.0 12.3 %collective-permute-start.55 = (f32[1024,128]{1,0:T(8,128)S(1)}, f32[1024,128]{1,0:T(8,128)S(1)}, u32[]{:S(2)}, u32[]{:S(2)}) collective-permute-start(f32[1024,128]{1,0:T(8,128)S(1)} %add.134), channel_id=1, source_target_pairs={{25,26},{26,25},{29,30},{30,29}} | collective-permute-start | bytes 1572872 | tf_op jit(solution)/shard_map/ppermute | solution.py:252
  (35 other events, 186.4 us)

commit v4 on v3

--- a/solution.py
+++ b/solution.py
@@ -304,6 +304,10 @@
     def rest(self, words, ahead, n_out, blocks):
         return panel_rest(self.role, self.meta, len(LEAVE), ahead, n_out, self.panel, self.mask, words, blocks)
 
+    def send_first(self, value, pairs, more=16):
+        rows = value.shape[0]
+        return self.send(jnp.pad(value, ((0, more), (0, 0))), pairs)[:rows]
+
     def both(self, inner, end):
         return jnp.where(self.inner, inner, end)
 
@@ -318,7 +322,7 @@
             self.blocks = order.note(late, early(self.meta, self.mask, 0), early(self.meta, self.mask, 1))
         else:
             mid_a, side_a, own_a = order.step(mid_a, side_a, own_a)
-        near_a, across_a = order.note(self.send(mid_a, INWARD), self.send(side_a, MIDDLE))
+        near_a, across_a = order.note(self.send_first(mid_a, INWARD), self.send(side_a, MIDDLE))
         tot_a = None if prepare else order.note(self.solve((0, 1), [[own_a], [side_a]], None))
         own_a, side_a, mid_a, near_a, across_a, raw_b = order.step(own_a, side_a, mid_a, near_a, across_a, raw_b)
         far_a = order.note(self.send(across_a, INWARD))
@@ -333,26 +337,35 @@
         mid_b, side_b, r0_a, words_a = order.step(mid_b, side_b, r0_a, words_a)
         near_b, across_b = order.note(self.send(self.both(mid_b, r0_a), EDGES), self.send(side_b, MIDDLE))
         r1_a, r2_a, rown_a = order.note(*self.rest(words_a, 1, 3, self.blocks[2:]))
-        across_b, r0_a, r1_a, near_b, own_b, side_b, mid_b = order.step(
-            across_b, r0_a, r1_a, near_b, own_b, side_b, mid_b
-        )
+        order.noted = ()
         far_b = order.note(self.send(self.both(across_b, r1_a), EDGES))
         got_a = order.note(self.send(r0_a + near_b, MIDDLE))
         tot_b = order.note(self.solve((0, 1, 2), [[own_b], [side_b], [mid_b, near_b]], None))
-        r2_a, got_a, r1_a, far_b, tot_b, across_b = order.step(r2_a, got_a, r1_a, far_b, tot_b, across_b)
+        order.noted = ()
         rs_a, rm_a = order.note(self.send(r2_a + got_a, EDGES), self.send(r1_a + far_b, MIDDLE))
         tot_b = self.last(across_b, far_b, tot_b)
         solved_b, words_b, r0_b = order.note(*self.first(tot_b, self.swap(tot_b)))
         r0_b, words_b, rown_a, rs_a, rm_a = order.step(r0_b, words_b, rown_a, rs_a, rm_a)
         sent_a = rown_a + rs_a + rm_a
-        near = order.note(self.send(r0_b, OUTWARD))
-        passed_a = passed(sent_a)
-        r1_b = order.note(*self.rest(words_b, 1, 1, self.blocks[2:]))
-        r0_b, near, r1_b, passed_a, words_b = order.step(r0_b, near, r1_b, passed_a, words_b)
-        far, got = order.note(self.send(r1_b, OUTWARD), self.send(r0_b + near, MIDDLE))
-        r2_b, rown_b = order.note(*self.rest(words_b, 2, 2, ()))
-        r2_b, got, r1_b, far = order.step(r2_b, got, r1_b, far)
-        rs_b, rm_b = self.send(r2_b + got, EDGES), self.send(r1_b + far, MIDDLE)
+        if prepare:
+            near = order.note(self.send(r0_b, OUTWARD))
+            passed_a = passed(sent_a)
+            r1_b = order.note(*self.rest(words_b, 1, 1, self.blocks[2:]))
+            r0_b, near, r1_b, passed_a, words_b = order.step(r0_b, near, r1_b, passed_a, words_b)
+            far, got = order.note(self.send_first(r1_b, OUTWARD), self.send(r0_b + near, MIDDLE))
+            r2_b, rown_b = order.note(*self.rest(words_b, 2, 2, ()))
+            r2_b, got, r1_b, far = order.step(r2_b, got, r1_b, far)
+            rs_b, rm_b = self.send_first(r2_b + got, EDGES), self.send(r1_b + far, MIDDLE)
+        else:
+            near = self.send_first(r0_b, OUTWARD, 64)
+            passed_a = passed(sent_a)
+            r1_b, = self.rest(words_b, 1, 1, self.blocks[2:])
+            far = self.send_first(r1_b, OUTWARD)
+            words_b, passed_a = lax.optimization_barrier((words_b, passed_a))
+            r2_b, rown_b = self.rest(words_b, 2, 2, ())
+            got = self.send(r0_b + near, MIDDLE)
+            rm_b = self.send(r1_b + far, MIDDLE)
+            rs_b = self.send(r2_b + got, EDGES)
         sent_b = rown_b + rs_b + rm_b
         return solved_a, sent_a, solved_b, sent_b, passed_a
 

time: 304 us -> 297 us (0.977)
  waiting for transfers between devices: 136 us -> 130 us
    ppermute x36, waiting for transfers between devices: 39 us -> 32.1 us  [send(): lax.ppermute(value, AXES, [(s * n + a, s * n + b) for s in secs for a, b...]
  transfers between devices with their start and end apart: 56 -> 56, of which waited for: 24 -> 21; matrix products, arithmetic and copies ran while one was open for 7% -> 8% of each run, Pallas kernels for 22% -> 22%
where the time goes in v4:
time: 297 us; the launch traced here: 296 us
  waiting for transfers between devices  130 us (44%)
  starting transfers between devices  70.6 us (24%)
  Pallas kernels  64.8 us (22%)
  local copies, waits for them, and re-layouts  13.8 us (5%)
  other arithmetic  12.4 us (4%)
  between operations  4.98 us (2%)
    ppermute x8, waiting for transfers between devices, hop(): lax.ppermute(value, AXES, [(a * n + c, b * n + c) for a, b in pairs for c...  89.5 us
    ppermute x36, starting transfers between devices, send(): lax.ppermute(value, AXES, [(s * n + a, s * n + b) for s in secs for a, b...  57.2 us
    ppermute x36, waiting for transfers between devices, send(): lax.ppermute(value, AXES, [(s * n + a, s * n + b) for s in secs for a, b...  32.1 us
    pallas_call x5, Pallas kernels, factor_pieces(): pl.pallas_call(functools.partial(pieces_body, role, pieces_at, counts, st...  25.1 us
    pallas_call x6, Pallas kernels, panel_rest(): pl.pallas_call(functools.partial(rest_body, role, ahead, len(blocks)), ou...  23.4 us
    ppermute x8, starting transfers between devices, hop(): lax.ppermute(value, AXES, [(a * n + c, b * n + c) for a, b in pairs for c...  10.5 us
    pallas_call x4, Pallas kernels, last_piece(): pl.pallas_call(functools.partial(last_body, role), out_shape=jax.ShapeDty...  8.45 us
    dynamic_slice x1, local copies, waits for them, and re-layouts, late(): lax.dynamic_slice(factor, (0, meta[ORDER + 3] * depth), (factor.shape[0],...  8.38 us
  transfers between devices with their start and end apart: 56, of which 21 were waited for; matrix products, arithmetic and copies ran while one was open for 8% of the time, Pallas kernels for 22%

profile of v4, /device:TPU:14, one launch (start us, length us, event | category | flops | bytes accessed | tf_op | source)
XLA Modules:
  0.0 296.1 jit_solution(7743893065343553689)
XLA Ops:
  6.5 8.4 %dynamic-slice_bitcast_fusion.block_ref = f32[2048,1024]{1,0:T(8,128)} fusion(f32[1,2048,4096]{2,1,0:T(8,128)} %param.6, s32[]{:T(128)S(6)} %select_n.62), kind=kLoop, calls=%fused_computation.2 | loop fusion | bytes 16777220 | tf_op jit(solution)/shard_map/dynamic_slice | solution.py:399
  20.3 7.0 %bitcast_multiply_fusion = (f32[1024,2048]{1,0:T(8,128)S(1)}, f32[1024,2048]{1,0:T(8,128)S(1)}) fusion(f32[1,4096,2048]{2,1,0:T(8,128)} %param.7, s32[]{:T(128)S(6)} %select_n.65, f32[8,2048]{1,0:T(8,128)S(1)} %get-tuple-element.176, f32[8,2048]{1,0:T(8,128)S(1)} %get-tuple-element.177, s32[]{:T(128)S(6)} %select_n.63), kind=kLoop, calls=%fused_computation | loop fusion | flops 4194304 | bytes 33685512 | tf_op jit(solution)/shard_map/mul | solution.py:404
  49.0 74.2 %collective-permute-done.20 = f32[512,128]{1,0:T(8,128)S(1)} collective-permute-done((f32[512,128]{1,0:T(8,128)S(1)}, f32[512,128]{1,0:T(8,128)S(1)}, u32[]{:S(2)}, u32[]{:S(2)}) %collective-permute-start.20) | collective-permute-done | bytes 262176 | tf_op jit(solution)/shard_map/ppermute | solution.py:257
  127.9 5.2 %collective-permute-done.21 = f32[512,128]{1,0:T(8,128)S(1)} collective-permute-done((f32[512,128]{1,0:T(8,128)S(1)}, f32[512,128]{1,0:T(8,128)S(1)}, u32[]{:S(2)}, u32[]{:S(2)}) %collective-permute-start.21) | collective-permute-done | bytes 262176 | tf_op jit(solution)/shard_map/ppermute | solution.py:257
  137.4 3.6 %collective-permute-start.24 = (f32[1024,128]{1,0:T(8,128)S(1)}, f32[1024,128]{1,0:T(8,128)S(1)}, u32[]{:S(2)}, u32[]{:S(2)}) collective-permute-start(f32[1024,128]{1,0:T(8,128)S(1)} %slice_subtract_fusion.refs_0_), channel_id=1, source_target_pairs={{25,26},{26,25},{29,30},{30,29}} | collective-permute-start | bytes 1572872 | tf_op jit(solution)/shard_map/ppermute | solution.py:252
  142.3 6.4 %collective-permute-done.25.refs_1_ = f32[1024,128]{1,0:T(8,128)S(1)} collective-permute-done((f32[1024,128]{1,0:T(8,128)S(1)}, f32[1024,128]{1,0:T(8,128)S(1)}, u32[]{:S(2)}, u32[]{:S(2)}) %collective-permute-start.25) | collective-permute-done | bytes 524320 | tf_op jit(solution)/shard_map/ppermute | solution.py:252
  154.1 3.6 %collective-permute-start.27 = (f32[1024,128]{1,0:T(8,128)S(1)}, f32[1024,128]{1,0:T(8,128)S(1)}, u32[]{:S(2)}, u32[]{:S(2)}) collective-permute-start(f32[1024,128]{1,0:T(8,128)S(1)} %collective-permute-done.25.refs_1_), channel_id=1, source_target_pairs={{25,26},{26,25},{29,30},{30,29}} | collective-permute-start | bytes 1572872 | tf_op jit(solution)/shard_map/ppermute | solution.py:252
  157.8 7.9 %shard_map.77.refs_2_ = f32[2048,128]{1,0:T(8,128)S(1)} custom-call(s32[11]{0:T(128)S(1)} %pad_add_fusion.meta, f32[2048,4096]{1,0:T(8,128)} %bitcast.50, f32[1024,128]{1,0:T(8,128)S(1)} %slice_subtract_fusion.refs_0_, f32[1024,128]{1,0:T(8,128)S(1)} %collective-permute-done.25.refs_1_), custom_call_target="tpu_custom_call" | custom-call | flops 1 | bytes 1 | tf_op jit(solution)/shard_map/pallas_call | solution.py:108
  171.0 4.3 %collective-permute-done.32 = f32[512,128]{1,0:T(8,128)S(1)} collective-permute-done((f32[512,128]{1,0:T(8,128)S(1)}, f32[512,128]{1,0:T(8,128)S(1)}, u32[]{:S(2)}, u32[]{:S(2)}) %collective-permute-start.32) | collective-permute-done | bytes 262176 | tf_op jit(solution)/shard_map/ppermute | solution.py:257
  179.6 5.4 %shard_map.78.total_ref = f32[2048,128]{1,0:T(8,128)S(1)} custom-call(s32[11]{0:T(128)S(1)} %pad_add_fusion.meta, f32[2048,4096]{1,0:T(8,128)} %bitcast.51, f32[1024,128]{1,0:T(8,128)S(1)} %collective-permute-done.24.refs_0_, f32[1024,128]{1,0:T(8,128)S(1)} %slice.122.refs_1_, f32[2048,128]{1,0:T(8,128)S(1)} %shard_map.77.refs_2_), custom_call_target="tpu_custom_call" | custom-call | flops 1 | bytes 1 | tf_op jit(solution)/shard_map/pallas_call | solution.py:108
  188.6 3.6 %collective-permute-start.40 = (f32[1024,128]{1,0:T(8,128)S(1)}, f32[1024,128]{1,0:T(8,128)S(1)}, u32[]{:S(2)}, u32[]{:S(2)}) collective-permute-start(f32[1024,128]{1,0:T(8,128)S(1)} %maximum_subtract_fusion.refs_0_), channel_id=1, source_target_pairs={{25,26},{26,25},{29,30},{30,29}} | collective-permute-start | bytes 1572872 | tf_op jit(solution)/shard_map/ppermute | solution.py:252
  192.2 3.6 %shard_map.79.mine_ref = f32[2048,128]{1,0:T(8,128)S(1)} custom-call(s32[11]{0:T(128)S(1)} %pad_add_fusion.meta, f32[2048,1024]{1,0:T(8,128)S(1)} %bitcast.34, f32[1024,128]{1,0:T(8,128)S(1)} %collective-permute-done.27.inner_ref, f32[1024,128]{1,0:T(8,128)S(1)} %collective-permute-done.36.end_ref, f32[2048,128]{1,0:T(8,128)S(1)} %shard_map.78.total_ref), custom_call_target="tpu_custom_call" | custom-call | flops 1 | bytes 1 | tf_op jit(solution)/shard_map/pallas_call | solution.py:139
  198.6 3.4 %shard_map.80 = (f32[2048,128]{1,0:T(8,128)S(1)}, bf16[2048,256]{1,0:T(8,128)(2,1)S(1)}, f32[1024,128]{1,0:T(8,128)S(1)}) custom-call(s32[11]{0:T(128)S(1)} %pad_add_fusion.meta, f32[1024,2048]{1,0:T(8,128)S(1)} %get-tuple-element.157.block_ref, f32[2048,128]{1,0:T(8,128)S(1)} %shard_map.79.mine_ref, f32[688,128]{1,0:T(8,128)S(1)} %collective-permute-done.37.refs_0_, ...), custom_call_target="tpu_custom_call" | custom-call | flops 1 | bytes 1 | tf_op jit(solution)/shard_map/pallas_call | solution.py:180
  206.7 9.8 %shard_map.81 = (f32[1024,128]{1,0:T(8,128)S(1)}, f32[1024,128]{1,0:T(8,128)S(1)}, f32[1024,128]{1,0:T(8,128)S(1)}) custom-call(s32[11]{0:T(128)S(1)} %pad_add_fusion.meta, f32[4096,2048]{1,0:T(8,128)} %bitcast.45, f32[32,2048]{1,0:T(8,128)S(1)} %bitcast.39, bf16[2048,256]{1,0:T(8,128)(2,1)S(1)} %get-tuple-element.137.words_ref, ...), custom_call_target="tpu_custom_call" | custom-call | flops 1 | bytes 1 | tf_op jit(solution)/shard_map/pallas_call | solution.py:239
  222.2 10.5 %shard_map.82.total_ref = f32[2048,128]{1,0:T(8,128)S(1)} custom-call(s32[11]{0:T(128)S(1)} %pad_add_fusion.meta, f32[2048,4096]{1,0:T(8,128)} %bitcast.52, f32[1024,128]{1,0:T(8,128)S(1)} %maximum_subtract_fusion.refs_0_, f32[1024,128]{1,0:T(8,128)S(1)} %collective-permute-done.41.refs_1_, f32[1024,128]{1,0:T(8,128)S(1)} %collective-permute-done.40.refs_2_, ...), custom_call_target="tpu_custom_call" | custom-call | flops 1 | bytes 1 | tf_op jit(solution)/shard_map/pallas_call | solution.py:108
  233.1 3.6 %collective-permute-start.49 = (f32[1024,128]{1,0:T(8,128)S(1)}, f32[1024,128]{1,0:T(8,128)S(1)}, u32[]{:S(2)}, u32[]{:S(2)}) collective-permute-start(f32[1024,128]{1,0:T(8,128)S(1)} %add.139), channel_id=1, source_target_pairs={{24,25},{25,24},{26,27},{27,26},{28,29},{29,28},{30,31},{31,30}} | collective-permute-start | bytes 1572872 | tf_op jit(solution)/shard_map/ppermute | solution.py:252
  236.8 3.6 %collective-permute-start.50 = (f32[1024,128]{1,0:T(8,128)S(1)}, f32[1024,128]{1,0:T(8,128)S(1)}, u32[]{:S(2)}, u32[]{:S(2)}) collective-permute-start(f32[1024,128]{1,0:T(8,128)S(1)} %add.140), channel_id=1, source_target_pairs={{25,26},{26,25},{29,30},{30,29}} | collective-permute-start | bytes 1572872 | tf_op jit(solution)/shard_map/ppermute | solution.py:252
  240.4 3.6 %shard_map.83.mine_ref = f32[2048,128]{1,0:T(8,128)S(1)} custom-call(s32[11]{0:T(128)S(1)} %pad_add_fusion.meta, f32[2048,1024]{1,0:T(8,128)S(1)} %bitcast.34, f32[1024,128]{1,0:T(8,128)S(1)} %collective-permute-done.42.inner_ref, f32[1024,128]{1,0:T(8,128)S(1)} %collective-permute-done.43.end_ref, f32[2048,128]{1,0:T(8,128)S(1)} %shard_map.82.total_ref), custom_call_target="tpu_custom_call" | custom-call | flops 1 | bytes 1 | tf_op jit(solution)/shard_map/pallas_call | solution.py:139
  246.8 3.4 %shard_map.84 = (f32[2048,128]{1,0:T(8,128)S(1)}, bf16[2048,256]{1,0:T(8,128)(2,1)S(1)}, f32[1024,128]{1,0:T(8,128)S(1)}) custom-call(s32[11]{0:T(128)S(1)} %pad_add_fusion.meta, f32[1024,2048]{1,0:T(8,128)S(1)} %get-tuple-element.157.block_ref, f32[2048,128]{1,0:T(8,128)S(1)} %shard_map.83.mine_ref, f32[688,128]{1,0:T(8,128)S(1)} %collective-permute-done.45.refs_0_, ...), custom_call_target="tpu_custom_call" | custom-call | flops 1 | bytes 1 | tf_op jit(solution)/shard_map/pallas_call | solution.py:180
  252.5 3.5 %shard_map.86 = f32[1024,128]{1,0:T(8,128)S(1)} custom-call(s32[11]{0:T(128)S(1)} %pad_add_fusion.meta, f32[4096,2048]{1,0:T(8,128)} %bitcast.46, f32[32,2048]{1,0:T(8,128)S(1)} %bitcast.40, bf16[2048,256]{1,0:T(8,128)(2,1)S(1)} %get-tuple-element.150.words_ref, f32[1024,2048]{1,0:T(8,128)S(1)} %get-tuple-element.156.refs_0_), custom_call_target="tpu_custom_call" | custom-call | flops 1 | bytes 1 | tf_op jit(solution)/shard_map/pallas_call | solution.py:239
  257.3 11.2 %collective-permute-done.51 = f32[1088,128]{1,0:T(8,128)S(1)} collective-permute-done((f32[1088,128]{1,0:T(8,128)S(1)}, f32[1088,128]{1,0:T(8,128)S(1)}, u32[]{:S(2)}, u32[]{:S(2)}) %collective-permute-start.51) | collective-permute-done | bytes 557088 | tf_op jit(solution)/shard_map/ppermute | solution.py:252
  268.6 3.6 %collective-permute-start.52 = (f32[1024,128]{1,0:T(8,128)S(1)}, f32[1024,128]{1,0:T(8,128)S(1)}, u32[]{:S(2)}, u32[]{:S(2)}) collective-permute-start(f32[1024,128]{1,0:T(8,128)S(1)} %slice_add_fusion.1), channel_id=1, source_target_pairs={{25,26},{26,25},{29,30},{30,29}} | collective-permute-start | bytes 1572872 | tf_op jit(solution)/shard_map/ppermute | solution.py:252
  272.3 8.3 %shard_map.85 = (f32[1024,128]{1,0:T(8,128)S(1)}, f32[1024,128]{1,0:T(8,128)S(1)}) custom-call(s32[11]{0:T(128)S(1)} %pad_add_fusion.meta, f32[4096,2048]{1,0:T(8,128)} %bitcast.47, f32[32,2048]{1,0:T(8,128)S(1)} %bitcast.41, bf16[2048,256]{1,0:T(8,128)(2,1)S(1)} %get-tuple-element.150.words_ref), custom_call_target="tpu_custom_call" | custom-call | flops 1 | bytes 1 | tf_op jit(solution)/shard_map/pallas_call | solution.py:239
  286.5 5.9 %collective-permute-done.55 = f32[1024,128]{1,0:T(8,128)S(1)} collective-permute-done((f32[1024,128]{1,0:T(8,128)S(1)}, f32[1024,128]{1,0:T(8,128)S(1)}, u32[]{:S(2)}, u32[]{:S(2)}) %collective-permute-start.55) | collective-permute-done | bytes 524320 | tf_op jit(solution)/shard_map/ppermute | solution.py:252
  (179 shorter events, 87.5 us)
Async XLA Ops:
  1.9 13.0 %collective-permute-start.1 = (f32[1024,128]{1,0:T(8,128)S(1)}, f32[1024,128]{1,0:T(8,128)S(1)}, u32[]{:S(2)}, u32[]{:S(2)}) collective-permute-start(f32[1024,128]{1,0:T(8,128)S(1)} %get-tuple-element.84.refs_0_), channel_id=1, source_target_pairs={{0,1},{1,0},{2,3},{3,2},{8,9},{9,8},{10,11},{11,10},{16,17},{17,16... | collective-permute-start | bytes 1572872 | tf_op jit(solution)/shard_map/ppermute | solution.py:252
  14.9 12.4 %collective-permute-start.2 = (f32[1040,128]{1,0:T(8,128)S(1)}, f32[1040,128]{1,0:T(8,128)}, u32[]{:S(2)}, u32[]{:S(2)}) collective-permute-start(f32[1040,128]{1,0:T(8,128)S(1)} %pad.20), channel_id=1, source_target_pairs={{1,0},{2,3},{9,8},{10,11},{17,16},{18,19},{5,4},{6,7},{13,12},{14,... | collective-permute-start | bytes 1597448 | tf_op jit(solution)/shard_map/ppermute | solution.py:252
  45.7 77.5 %collective-permute-start.20 = (f32[512,128]{1,0:T(8,128)S(1)}, f32[512,128]{1,0:T(8,128)S(1)}, u32[]{:S(2)}, u32[]{:S(2)}) collective-permute-start(f32[512,128]{1,0:T(8,128)S(1)} %get-tuple-element.174), channel_id=1, source_target_pairs={{0,8},{1,9},{2,10},{3,11},{16,24},{17,25},{18,26},{19,27},{4,12},{... | collective-permute-start | bytes 786440 | tf_op jit(solution)/shard_map/ppermute | solution.py:257
  47.0 77.4 %collective-permute-start.22 = (f32[512,128]{1,0:T(8,128)S(1)}, f32[512,128]{1,0:T(8,128)S(1)}, u32[]{:S(2)}, u32[]{:S(2)}) collective-permute-start(f32[512,128]{1,0:T(8,128)S(1)} %get-tuple-element.175), channel_id=1, source_target_pairs={{0,16},{1,17},{2,18},{3,19},{8,24},{9,25},{10,26},{11,27},{4,20},{... | collective-permute-start | bytes 786440 | tf_op jit(solution)/shard_map/ppermute | solution.py:257
  48.3 86.3 %collective-permute-start.19 = (f32[1024,128]{1,0:T(8,128)S(1)}, f32[1024,128]{1,0:T(8,128)S(1)}, u32[]{:S(2)}, u32[]{:S(2)}) collective-permute-start(f32[1024,128]{1,0:T(8,128)S(1)} %get-tuple-element.118), channel_id=1, source_target_pairs={{0,1},{3,2},{8,9},{11,10},{16,17},{19,18},{4,5},{7,6},{12,13},{15,... | collective-permute-start | bytes 1572872 | tf_op jit(solution)/shard_map/ppermute | solution.py:252
  134.7 17.8 %collective-permute-start.29 = (f32[1040,128]{1,0:T(8,128)S(1)}, f32[1040,128]{1,0:T(8,128)S(1)}, u32[]{:S(2)}, u32[]{:S(2)}) collective-permute-start(f32[1040,128]{1,0:T(8,128)S(1)} %pad.22), channel_id=1, source_target_pairs={{0,1},{3,2},{8,9},{11,10},{16,17},{19,18},{4,5},{7,6},{12,13},{15,... | collective-permute-start | bytes 1597448 | tf_op jit(solution)/shard_map/ppermute | solution.py:252
  135.4 13.3 %collective-permute-start.25 = (f32[1024,128]{1,0:T(8,128)S(1)}, f32[1024,128]{1,0:T(8,128)S(1)}, u32[]{:S(2)}, u32[]{:S(2)}) collective-permute-start(f32[1024,128]{1,0:T(8,128)S(1)} %slice_subtract_fusion.refs_0_), channel_id=1, source_target_pairs={{24,25},{25,24},{26,27},{27,26},{28,29},{29,28},{30,31},{31,30}} | collective-permute-start | bytes 1572872 | tf_op jit(solution)/shard_map/ppermute | solution.py:252
  137.4 13.7 %collective-permute-start.24 = (f32[1024,128]{1,0:T(8,128)S(1)}, f32[1024,128]{1,0:T(8,128)S(1)}, u32[]{:S(2)}, u32[]{:S(2)}) collective-permute-start(f32[1024,128]{1,0:T(8,128)S(1)} %slice_subtract_fusion.refs_0_), channel_id=1, source_target_pairs={{25,26},{26,25},{29,30},{30,29}} | collective-permute-start | bytes 1572872 | tf_op jit(solution)/shard_map/ppermute | solution.py:252
  151.1 14.6 %collective-permute-start.26 = (f32[1040,128]{1,0:T(8,128)S(1)}, f32[1040,128]{1,0:T(8,128)S(1)}, u32[]{:S(2)}, u32[]{:S(2)}) collective-permute-start(f32[1040,128]{1,0:T(8,128)S(1)} %pad.21), channel_id=1, source_target_pairs={{25,24},{26,27},{29,28},{30,31}} | collective-permute-start | bytes 1597448 | tf_op jit(solution)/shard_map/ppermute | solution.py:252
  152.6 13.1 %collective-permute-start.30 = (f32[1040,128]{1,0:T(8,128)S(1)}, f32[1040,128]{1,0:T(8,128)S(1)}, u32[]{:S(2)}, u32[]{:S(2)}) collective-permute-start(f32[1040,128]{1,0:T(8,128)S(1)} %pad.23), channel_id=1, source_target_pairs={{0,1},{1,0},{2,3},{3,2},{8,9},{9,8},{10,11},{11,10},{16,17},{17,16... | collective-permute-start | bytes 1597448 | tf_op jit(solution)/shard_map/ppermute | solution.py:252
  153.4 12.3 %collective-permute-start.31 = (f32[1024,128]{1,0:T(8,128)S(1)}, f32[1024,128]{1,0:T(8,128)S(1)}, u32[]{:S(2)}, u32[]{:S(2)}) collective-permute-start(f32[1024,128]{1,0:T(8,128)S(1)} %add.132), channel_id=1, source_target_pairs={{1,2},{2,1},{9,10},{10,9},{17,18},{18,17},{5,6},{6,5},{13,14},{14,... | collective-permute-start | bytes 1572872 | tf_op jit(solution)/shard_map/ppermute | solution.py:252
  154.1 12.9 %collective-permute-start.27 = (f32[1024,128]{1,0:T(8,128)S(1)}, f32[1024,128]{1,0:T(8,128)S(1)}, u32[]{:S(2)}, u32[]{:S(2)}) collective-permute-start(f32[1024,128]{1,0:T(8,128)S(1)} %collective-permute-done.25.refs_1_), channel_id=1, source_target_pairs={{25,26},{26,25},{29,30},{30,29}} | collective-permute-start | bytes 1572872 | tf_op jit(solution)/shard_map/ppermute | solution.py:252
  169.6 17.0 %collective-permute-start.36 = (f32[1024,128]{1,0:T(8,128)S(1)}, f32[1024,128]{1,0:T(8,128)S(1)}, u32[]{:S(2)}, u32[]{:S(2)}) collective-permute-start(f32[1024,128]{1,0:T(8,128)S(1)} %collective-permute-done.27.inner_ref), channel_id=1, source_target_pairs={{25,24},{26,27},{29,28},{30,31}} | collective-permute-start | bytes 1572872 | tf_op jit(solution)/shard_map/ppermute | solution.py:252
  186.7 15.3 %collective-permute-start.41 = (f32[1024,128]{1,0:T(8,128)S(1)}, f32[1024,128]{1,0:T(8,128)S(1)}, u32[]{:S(2)}, u32[]{:S(2)}) collective-permute-start(f32[1024,128]{1,0:T(8,128)S(1)} %maximum_subtract_fusion.refs_0_), channel_id=1, source_target_pairs={{24,25},{25,24},{26,27},{27,26},{28,29},{29,28},{30,31},{31,30}} | collective-permute-start | bytes 1572872 | tf_op jit(solution)/shard_map/ppermute | solution.py:252
  188.6 13.4 %collective-permute-start.40 = (f32[1024,128]{1,0:T(8,128)S(1)}, f32[1024,128]{1,0:T(8,128)S(1)}, u32[]{:S(2)}, u32[]{:S(2)}) collective-permute-start(f32[1024,128]{1,0:T(8,128)S(1)} %maximum_subtract_fusion.refs_0_), channel_id=1, source_target_pairs={{25,26},{26,25},{29,30},{30,29}} | collective-permute-start | bytes 1572872 | tf_op jit(solution)/shard_map/ppermute | solution.py:252
  202.1 15.9 %collective-permute-start.44 = (f32[1024,128]{1,0:T(8,128)S(1)}, f32[1024,128]{1,0:T(8,128)S(1)}, u32[]{:S(2)}, u32[]{:S(2)}) collective-permute-start(f32[1024,128]{1,0:T(8,128)S(1)} %broadcast_select_fusion.3), channel_id=1, source_target_pairs={{24,25},{25,24},{26,27},{27,26},{28,29},{29,28},{30,31},{31,30}} | collective-permute-start | bytes 1572872 | tf_op jit(solution)/shard_map/ppermute | solution.py:252
  204.0 16.2 %collective-permute-start.42 = (f32[1024,128]{1,0:T(8,128)S(1)}, f32[1024,128]{1,0:T(8,128)S(1)}, u32[]{:S(2)}, u32[]{:S(2)}) collective-permute-start(f32[1024,128]{1,0:T(8,128)S(1)} %collective-permute-done.41.refs_1_), channel_id=1, source_target_pairs={{25,26},{26,25},{29,30},{30,29}} | collective-permute-start | bytes 1572872 | tf_op jit(solution)/shard_map/ppermute | solution.py:252
  218.0 15.0 %collective-permute-start.48 = (f32[1024,128]{1,0:T(8,128)S(1)}, f32[1024,128]{1,0:T(8,128)S(1)}, u32[]{:S(2)}, u32[]{:S(2)}) collective-permute-start(f32[1024,128]{1,0:T(8,128)S(1)} %add.138), channel_id=1, source_target_pairs={{25,26},{26,25},{29,30},{30,29}} | collective-permute-start | bytes 1572872 | tf_op jit(solution)/shard_map/ppermute | solution.py:252
  220.3 16.4 %collective-permute-start.43 = (f32[1024,128]{1,0:T(8,128)S(1)}, f32[1024,128]{1,0:T(8,128)S(1)}, u32[]{:S(2)}, u32[]{:S(2)}) collective-permute-start(f32[1024,128]{1,0:T(8,128)S(1)} %broadcast_select_fusion.4), channel_id=1, source_target_pairs={{24,25},{25,24},{26,27},{27,26},{28,29},{29,28},{30,31},{31,30}} | collective-permute-start | bytes 1572872 | tf_op jit(solution)/shard_map/ppermute | solution.py:252
  233.1 17.1 %collective-permute-start.49 = (f32[1024,128]{1,0:T(8,128)S(1)}, f32[1024,128]{1,0:T(8,128)S(1)}, u32[]{:S(2)}, u32[]{:S(2)}) collective-permute-start(f32[1024,128]{1,0:T(8,128)S(1)} %add.139), channel_id=1, source_target_pairs={{24,25},{25,24},{26,27},{27,26},{28,29},{29,28},{30,31},{31,30}} | collective-permute-start | bytes 1572872 | tf_op jit(solution)/shard_map/ppermute | solution.py:252
  236.8 14.3 %collective-permute-start.50 = (f32[1024,128]{1,0:T(8,128)S(1)}, f32[1024,128]{1,0:T(8,128)S(1)}, u32[]{:S(2)}, u32[]{:S(2)}) collective-permute-start(f32[1024,128]{1,0:T(8,128)S(1)} %add.140), channel_id=1, source_target_pairs={{25,26},{26,25},{29,30},{30,29}} | collective-permute-start | bytes 1572872 | tf_op jit(solution)/shard_map/ppermute | solution.py:252
  251.1 17.5 %collective-permute-start.51 = (f32[1088,128]{1,0:T(8,128)S(1)}, f32[1088,128]{1,0:T(8,128)S(1)}, u32[]{:S(2)}, u32[]{:S(2)}) collective-permute-start(f32[1088,128]{1,0:T(8,128)S(1)} %pad.24), channel_id=1, source_target_pairs={{24,25},{27,26},{28,29},{31,30}} | collective-permute-start | bytes 1671176 | tf_op jit(solution)/shard_map/ppermute | solution.py:252
  256.0 24.6 %collective-permute-start.54 = (f32[1040,128]{1,0:T(8,128)S(1)}, f32[1040,128]{1,0:T(8,128)S(1)}, u32[]{:S(2)}, u32[]{:S(2)}) collective-permute-start(f32[1040,128]{1,0:T(8,128)S(1)} %pad.25), channel_id=1, source_target_pairs={{24,25},{27,26},{28,29},{31,30}} | collective-permute-start | bytes 1597448 | tf_op jit(solution)/shard_map/ppermute | solution.py:252
  268.6 14.4 %collective-permute-start.52 = (f32[1024,128]{1,0:T(8,128)S(1)}, f32[1024,128]{1,0:T(8,128)S(1)}, u32[]{:S(2)}, u32[]{:S(2)}) collective-permute-start(f32[1024,128]{1,0:T(8,128)S(1)} %slice_add_fusion.1), channel_id=1, source_target_pairs={{25,26},{26,25},{29,30},{30,29}} | collective-permute-start | bytes 1572872 | tf_op jit(solution)/shard_map/ppermute | solution.py:252
  (35 other events, 186.6 us)
